TPU v7x, 32 devices: a whole 2x2x4 slice. The times are simulated.
32 devices in a mesh: dp: 8 (over z, y), rep: 4 (over x, core).
Axes of the slice: x: 2, y: 2, z: 4, core: 2. Of those that a mesh axis runs over, the one named last changes fastest.
Arguments:
- mentions: bfloat16 [4096, 1024], P(('dp', 'rep')), may hold values from -48 to 48
- entity_states: bfloat16 [4096, 1024], P(('dp', 'rep')), may hold values from -8 to 8
- head: bfloat16 [1024, 1024], P('dp'), may hold values from -4 to 4
Outputs:
- pair_loss: float32 [4096], P(('dp', 'rep'))
- mention_grad: bfloat16 [4096, 1024], P(('dp', 'rep'))
- state_grad: bfloat16 [4096, 1024], P(('dp', 'rep'))
All inputs are finite; a program needn't handle non-finite values.
Results may differ from a plain program's by a relative error of at most 0.0073.
Values may be sent and summed in bfloat16 or wider, within the bound.
No kernel may reach another device: no remote copies, remote signals or barrier semaphores. Data moves between devices by JAX's collectives and lax.ppermute only.
A program may use at most 64 MiB of HBM per device.

v0:
```python
import math

import jax
import jax.numpy as jnp
from jax import lax
from jax.sharding import PartitionSpec as P


def local(mentions, entity_states, head):
    row_count, feature_count = mentions.shape
    scale_factor = 3.0 / math.sqrt(feature_count)
    contract = (((1,), (1,)), ((), ()))

    def score(left_rows, right_rows):
        return (
            lax.dot_general(left_rows, right_rows, contract, preferred_element_type=jnp.float32)
            * scale_factor
        )

    weights = lax.all_gather(head, "dp", axis=0, tiled=True)
    projected = jnp.dot(entity_states, weights, preferred_element_type=jnp.float32).astype(
        jnp.bfloat16
    )
    matched = (
        jnp.einsum("rd,rd->r", mentions, projected, preferred_element_type=jnp.float32)
        * scale_factor
    )
    gathered = lax.all_gather(projected, "rep", axis=0, tiled=True)
    scores = score(mentions, gathered)
    row_max = jnp.max(scores, axis=1)
    log_total = row_max + jnp.log(jnp.sum(jnp.exp(scores - row_max[:, None]), axis=1))
    chances = jnp.exp(scores - log_total[:, None]).astype(jnp.bfloat16)
    weighted = jnp.dot(chances, gathered, preferred_element_type=jnp.float32)
    pair_loss = log_total - matched
    mention_grad = (scale_factor * (weighted - projected.astype(jnp.float32))).astype(jnp.bfloat16)
    totals = lax.all_gather(log_total, "rep", axis=0, tiled=True)
    portion = lax.all_gather(mentions, "rep", axis=0, tiled=True)
    scores = score(portion, projected)
    chances = jnp.exp(scores - totals[:, None]).astype(jnp.bfloat16)
    summed = lax.dot_general(
        chances, portion, (((0,), (0,)), ((), ())), preferred_element_type=jnp.float32
    )
    proj_grad = (scale_factor * (summed - mentions.astype(jnp.float32))).astype(jnp.bfloat16)
    state_grad = lax.dot_general(
        proj_grad, weights, contract, preferred_element_type=jnp.float32
    ).astype(jnp.bfloat16)
    return (pair_loss, mention_grad, state_grad)


def solution(mesh):
    placed = (P(("dp", "rep"), None), P(("dp", "rep"), None), P("dp", None))
    return jax.shard_map(
        local,
        mesh=mesh,
        in_specs=placed,
        out_specs=(P(("dp", "rep")), P(("dp", "rep"), None), P(("dp", "rep"), None)),
        check_vma=False,
    )
```

profile of v0, /device:TPU:0, one launch (start us, length us, event | category | flops | bytes accessed | tf_op | source)
XLA Modules:
  0.0 109.8 jit_solution(6724306989615766550)
XLA Ops:
  7.2 0.0 copy-start
  7.2 0.0 copy-start.4
  7.2 0.0 all-gather.5.cloned.1.call-start
  7.2 0.7 all-gather.5.cloned.1.call-update
  7.9 0.0 all-gather.7.cloned.1.call-start
  8.0 54.2 %all-gather.5.cloned.1.call-done = bf16[1024,1024]{1,0:T(8,128)(2,1)} async-done(((bf16[128,1024]{1,0:T(8,128)(2,1)}), bf16[1024,1024]{1,0:T(8,128)(2,1)}) %all-gather.5.cloned.1.call-update) | async-done | bytes 2097168 | tf_op jit(solution)/shard_map/all_gather | solution.py:20
  62.2 0.0 copy-done
  62.2 2.7 %fusion.8 = (f32[128]{0:T(128)S(1)}, bf16[128,1024]{1,0:T(8,128)(2,1)}) fusion(bf16[128,1024]{1,0:T(8,128)(2,1)} %param.3, bf16[128,1024]{1,0:T(8,128)(2,1)S(1)} %copy-done, bf16[1024,1024]{1,0:T(8,128)(2,1)} %all-gather.5.cloned.1.call-done), kind=kOutput, calls=%fused_computation.15 | convolution fusion | flops 269090688 | bytes 2884096 | tf_op jit(solution)/shard_map/dot_general | solution.py:21
  64.9 0.0 copy-start.3
  64.9 0.0 all-gather.7.cloned.1.call-update
  64.9 0.0 all-gather.9.cloned.1.call-start
  65.0 0.7 all-gather.9.cloned.1.call-update
  65.7 14.6 %all-gather.7.cloned.1.call-done = bf16[512,1024]{1,0:T(8,128)(2,1)} async-done(((bf16[128,1024]{1,0:T(8,128)(2,1)}), bf16[512,1024]{1,0:T(8,128)(2,1)}) %all-gather.7.cloned.1.call-update) | async-done | bytes 1048592 | tf_op jit(solution)/shard_map/all_gather | solution.py:28
  80.3 0.0 copy-done.4
  80.3 0.0 copy-start.2
  80.3 1.8 %fusion.12 = (f32[128]{0:T(128)S(1)}, f32[512,128]{1,0:T(8,128)S(1)}) fusion(bf16[512,1024]{1,0:T(8,128)(2,1)} %all-gather.7.cloned.1.call-done, bf16[128,1024]{1,0:T(8,128)(2,1)S(1)} %copy-done.4), kind=kOutput, calls=%fused_computation.23 | convolution fusion | flops 134348672 | bytes 1573376 | tf_op jit(solution)/shard_map/dot_general | solution.py:16
  82.1 0.0 copy-start.1
  82.1 0.1 exponential_reduce_fusion
  82.2 0.5 multiply_subtract_fusion
  82.7 5.2 %all-gather = f32[4,1,128]{2,1,0:T(1,128)S(1)} all-gather(f32[1,1,128]{2,1,0:T(1,128)S(1)} %bitcast.13), channel_id=1, replica_groups=mesh['dp'=8,'rep'=4] {'rep'}, dimensions={0}, use_global_device_ids=true | all-gather | bytes 2560 | tf_op jit(solution)/shard_map/all_gather | solution.py:36
  87.9 0.0 copy-done.3
  87.9 0.0 copy-done.2
  87.9 1.0 fusion.3
  88.9 9.7 %all-gather.9.cloned.1.call-done = bf16[512,1024]{1,0:T(8,128)(2,1)} async-done(((bf16[128,1024]{1,0:T(8,128)(2,1)}), bf16[512,1024]{1,0:T(8,128)(2,1)}) %all-gather.9.cloned.1.call-update) | async-done | bytes 1048592 | tf_op jit(solution)/shard_map/all_gather | solution.py:37
  98.6 1.7 %fusion.6 = bf16[128,512]{1,0:T(8,128)(2,1)S(1)} fusion(bf16[128,1024]{1,0:T(8,128)(2,1)S(1)} %copy-done.3, bf16[512,1024]{1,0:T(8,128)(2,1)} %all-gather.9.cloned.1.call-done, f32[512]{0:T(512)S(1)} %bitcast.12), kind=kOutput, calls=%fused_computation.12 | convolution fusion | flops 134414336 | bytes 1443840 | tf_op jit(solution)/shard_map/dot_general | solution.py:16
  100.4 0.0 copy-done.1
  100.4 2.9 %convolution_convert_fusion = bf16[128,1024]{1,0:T(8,128)(2,1)} fusion(bf16[1024,1024]{1,0:T(8,128)(2,1)S(1)} %copy-done.1, bf16[128,512]{1,0:T(8,128)(2,1)S(1)} %fusion.6, bf16[512,1024]{1,0:T(8,128)(2,1)} %all-gather.9.cloned.1.call-done, bf16[128,1024]{1,0:T(8,128)(2,1)S(1)} %copy-done.4), kind=kOutput, calls=%fused_computation.6 | convolution fusion | flops 403308544 | bytes 3801088 | tf_op jit(solution)/shard_map/dot_general | solution.py:44
Async XLA Ops:
  7.2 55.0 %copy-start = (bf16[128,1024]{1,0:T(8,128)(2,1)S(1)}, bf16[128,1024]{1,0:T(8,128)(2,1)}, u32[]{:S(2)}) copy-start(bf16[128,1024]{1,0:T(8,128)(2,1)} %param.4) | copy-start | bytes 786436
  7.2 73.1 %copy-start.4 = (bf16[128,1024]{1,0:T(8,128)(2,1)S(1)}, bf16[128,1024]{1,0:T(8,128)(2,1)}, u32[]{:S(2)}) copy-start(bf16[128,1024]{1,0:T(8,128)(2,1)} %param.3) | copy-start | bytes 786436
  7.2 55.0 %all-gather.5.cloned.1.call-start = ((), (), s32[]{:S(2)}) async-start(), calls=%async_computation | async-start | bytes 2359296 | tf_op jit(solution)/shard_map/all_gather | solution.py:20
  7.9 72.4 %all-gather.7.cloned.1.call-start = ((), (), s32[]{:S(2)}) async-start(), calls=%async_computation.1 | async-start | bytes 1310720 | tf_op jit(solution)/shard_map/all_gather | solution.py:28
  64.9 22.9 %copy-start.3 = (bf16[128,1024]{1,0:T(8,128)(2,1)S(1)}, bf16[128,1024]{1,0:T(8,128)(2,1)}, u32[]{:S(2)}) copy-start(bf16[128,1024]{1,0:T(8,128)(2,1)} %get-tuple-element.6) | copy-start | bytes 786436
  64.9 33.7 %all-gather.9.cloned.1.call-start = ((), (), s32[]{:S(2)}) async-start(), calls=%async_computation.2 | async-start | bytes 1310720 | tf_op jit(solution)/shard_map/all_gather | solution.py:37
  80.3 7.6 %copy-start.2 = (bf16[512,1024]{1,0:T(8,128)(2,1)S(1)}, bf16[512,1024]{1,0:T(8,128)(2,1)}, u32[]{:S(2)}) copy-start(bf16[512,1024]{1,0:T(8,128)(2,1)} %all-gather.7.cloned.1.call-done) | copy-start | bytes 3145732
  82.1 18.3 %copy-start.1 = (bf16[1024,1024]{1,0:T(8,128)(2,1)S(1)}, bf16[1024,1024]{1,0:T(8,128)(2,1)}, u32[]{:S(2)}) copy-start(bf16[1024,1024]{1,0:T(8,128)(2,1)} %all-gather.5.cloned.1.call-done) | copy-start | bytes 6291460
Sparse Core Ops, SparseCore 0:
  10.1 51.9 all-gather.4
  65.1 15.1 all-gather.6
  81.9 16.7 all-gather.8
where the time goes:
time: 110 us
  waiting for transfers between devices  79.9 us (73%)
  between operations  13.8 us (13%)
  matrix products  10.2 us (9%)
  blocking collectives  5.16 us (5%)
    all_gather x1, waiting for transfers between devices, local(): weights = lax.all_gather(head, 'dp', axis=0, tiled=True)  54.2 us
    all_gather x1, waiting for transfers between devices, local(): gathered = lax.all_gather(projected, 'rep', axis=0, tiled=True)  14.6 us
    all_gather x1, waiting for transfers between devices, local(): portion = lax.all_gather(mentions, 'rep', axis=0, tiled=True)  9.72 us
    all_gather x1, blocking collectives, local(): totals = lax.all_gather(log_total, 'rep', axis=0, tiled=True)  5.16 us
    dot_general x2, matrix products, score(): lax.dot_general(left_rows, right_rows, contract, preferred_element_type=j...  3.49 us
    dot_general x1, matrix products, local(): lax.dot_general(proj_grad, weights, contract, preferred_element_type=jnp....  2.93 us
    dot_general x1, matrix products, local(): jnp.dot(entity_states, weights, preferred_element_type=jnp.float32)  2.75 us
  transfers between devices with their start and end apart: 3, of which 3 were waited for; matrix products, arithmetic and copies ran while one was open for 3% of the time, Pallas kernels for 0%

commit v1 on v0

v1 whole, which is shorter than its diff:
```python
import functools
import math

import jax
import jax.numpy as jnp
from jax import lax
from jax.experimental import pallas as pl
from jax.experimental.pallas import tpu as pltpu
from jax.sharding import PartitionSpec as P

LAST = (((1,), (1,)), ((), ()))
FIRST = (((0,), (0,)), ((), ()))


def dot(left, right, contract=(((1,), (0,)), ((), ()))):
    return lax.dot_general(left, right, contract, preferred_element_type=jnp.float32)


def kernel(dp, rep, scale, *refs):
    head_ref, refs = refs[0], refs[1:]
    mine_refs, refs = refs[: dp - 1], refs[dp - 1 :]
    theirs_refs, refs = refs[: dp - 1], refs[dp - 1 :]
    entity_refs, refs = refs[:rep], refs[rep:]
    mention_refs, refs = refs[:rep], refs[rep:]
    loss_ref, mention_grad_ref, state_grad_ref = refs[:3]
    head, entities, mentions, projected, sems = refs[3:]

    rows = entity_refs[0].shape[0]
    depth, half = head_ref.shape[0], mine_refs[0].shape[1]
    me, core = lax.axis_index("dp"), lax.rem(lax.axis_index("rep"), 2)

    copies = []

    def fetch(source, target):
        copy = pltpu.make_async_copy(source, target, sems.at[len(copies)])
        copy.start()
        copies.append(copy)

    def place(mask, column):
        at = pl.multiple_of(jnp.bitwise_xor(me, mask) * depth, depth)
        return head.at[pl.ds(at, depth), pl.ds(pl.multiple_of(column * half, half), half)]

    for i in range(rep):
        fetch(entity_refs[i], entities.at[pl.ds(i * rows, rows)])
    fetch(head_ref, head.at[pl.ds(pl.multiple_of(me * depth, depth), depth)])
    for mask in range(1, dp):
        fetch(mine_refs[mask - 1], place(mask, core))
        fetch(theirs_refs[mask - 1], place(mask, 1 - core))
    ready = len(copies)
    for i in range(rep):
        fetch(mention_refs[i], mentions.at[pl.ds(i * rows, rows)])

    for copy in copies[:ready]:
        copy.wait()
    group, width = projected.shape
    step = 256
    for at in range(0, width, step):
        projected[:, at : at + step] = dot(entities[...], head[:, at : at + step]).astype(jnp.bfloat16)
    for copy in copies[ready:]:
        copy.wait()

    block = min(group, 512)
    summed = jnp.zeros((rows, width), jnp.float32)
    for at in range(0, group, block):
        part = mentions[at : at + block, :]
        scores = dot(part, projected[...], LAST) * scale
        top = jnp.max(scores, axis=1, keepdims=True)
        powers = jnp.exp(scores - top)
        total = jnp.sum(powers, axis=1, keepdims=True)
        chances = (powers / total).astype(jnp.bfloat16)
        summed += dot(chances[:, :rows], part, FIRST)
        if at == 0:
            log_total = top[:rows] + jnp.log(total[:rows])
            eye = lax.broadcasted_iota(jnp.int32, (rows, rows), 0) == lax.broadcasted_iota(
                jnp.int32, (rows, rows), 1
            )
            losses = jnp.where(eye, log_total - scores[:rows, :rows], 0.0)
            loss_ref[...] = jnp.sum(losses, axis=0)
            weighted = dot(chances[:rows], projected[...])
            mention_grad_ref[...] = (
                scale * (weighted - projected[:rows, :].astype(jnp.float32))
            ).astype(jnp.bfloat16)
    proj_grad = (scale * (summed - mentions[:rows, :].astype(jnp.float32))).astype(jnp.bfloat16)
    state_grad_ref[...] = dot(proj_grad, head[...], LAST).astype(jnp.bfloat16)


def solution(mesh):
    dp, rep = mesh.shape["dp"], mesh.shape["rep"]

    def send(x, over_dp, over_rep):
        pairs = [
            (d * rep + r, (d ^ over_dp) * rep + (r ^ over_rep)) for d in range(dp) for r in range(rep)
        ]
        return lax.ppermute(x, ("dp", "rep"), pairs)

    def local(mentions, entity_states, head):
        rows, width = mentions.shape
        half = width // 2
        core = lax.rem(lax.axis_index("rep"), 2)
        own = lax.dynamic_slice_in_dim(head, core * half, half, axis=1)

        mine = {}
        for mask in range(2, dp, 2):
            mine[mask] = send(own, mask, 0)
        mine[1] = send(own, 1, 0)
        entities, held = {0: entity_states}, {0: mentions}
        for store in (entities, held):
            for mask in range(2, rep, 2):
                store[mask] = send(store[0], 0, mask)
            for mask in range(0, rep, 2):
                store[mask + 1] = send(store[mask], 0, 1)
        for mask in range(2, dp, 2):
            mine[mask + 1] = send(mine[mask], 1, 0)
        theirs = {mask: send(mine[mask], 0, 1) for mask in range(1, dp)}

        operands = (
            [head]
            + [mine[i] for i in range(1, dp)]
            + [theirs[i] for i in range(1, dp)]
            + [entities[i] for i in range(rep)]
            + [held[i] for i in range(rep)]
        )
        group = rep * rows
        anywhere = pl.BlockSpec(memory_space=pl.ANY)
        vmem = pl.BlockSpec(memory_space=pltpu.VMEM)
        return pl.pallas_call(
            functools.partial(kernel, dp, rep, 3.0 / math.sqrt(width)),
            out_shape=(
                jax.ShapeDtypeStruct((rows,), jnp.float32),
                jax.ShapeDtypeStruct((rows, width), jnp.bfloat16),
                jax.ShapeDtypeStruct((rows, width), jnp.bfloat16),
            ),
            in_specs=[anywhere] * len(operands),
            out_specs=(vmem, vmem, vmem),
            scratch_shapes=[
                pltpu.VMEM((dp * head.shape[0], width), jnp.bfloat16),
                pltpu.VMEM((group, width), jnp.bfloat16),
                pltpu.VMEM((group, width), jnp.bfloat16),
                pltpu.VMEM((group, width), jnp.bfloat16),
                pltpu.SemaphoreType.DMA((len(operands),)),
            ],
            compiler_params=pltpu.CompilerParams(vmem_limit_bytes=48 * 1024 * 1024),
            name="group_softmax",
        )(*operands)

    return jax.shard_map(
        local,
        mesh=mesh,
        in_specs=(P(("dp", "rep"), None), P(("dp", "rep"), None), P("dp", None)),
        out_specs=(P(("dp", "rep")), P(("dp", "rep"), None), P(("dp", "rep"), None)),
        check_vma=False,
    )
```

time: 110 us -> 41.2 us (0.37)
  waiting for transfers between devices: 79.9 us -> 17.5 us
  starting transfers between devices: 0.12 us -> 15.3 us
  between operations: 13.8 us -> 0.69 us
  matrix products: 10.2 us -> 0 us
  blocking collectives: 5.16 us -> 0 us
  Pallas kernels: 0 us -> 4.64 us
  local copies, waits for them, and re-layouts: 0.02 us -> 2.87 us
    all_gather x3 -> x0, waiting for transfers between devices: 78.5 us -> none  [the longest x1 54.2 us: local(): weights = lax.all_gather(head, 'dp', axis=0, tiled=True)]
    ppermute x0 -> x20, waiting for transfers between devices: none -> 17.5 us  [send(): return lax.ppermute(x, ('dp', 'rep'), pairs)]
    ppermute x0 -> x20, starting transfers between devices: none -> 15.3 us  [send(): return lax.ppermute(x, ('dp', 'rep'), pairs)]
    dot_general x5 -> x0, matrix products: 10.2 us -> none  [the longest x2 3.49 us: score(): lax.dot_general(left_rows, right_rows, contract, preferred_element_type=j...]
    all_gather x1 -> x0, blocking collectives: 5.16 us -> none  [local(): totals = lax.all_gather(log_total, 'rep', axis=0, tiled=True)]
    pallas_call x0 -> x1, Pallas kernels: none -> 4.64 us  [local(): pl.pallas_call(functools.partial(kernel, dp, rep, 3.0 / math.sqrt(width))...]
    unnamed x10 -> x6, local copies, waits for them, and re-layouts: 0.02 us -> 1.9 us
    unnamed x3 -> x0, waiting for transfers between devices: 1.38 us -> none
  transfers between devices with their start and end apart: 3 -> 20, of which waited for: 3 -> 8; matrix products, arithmetic and copies ran while one was open for 3% -> 0% of each run, Pallas kernels for 0% -> 0%
where the time goes in v1:
time: 41.2 us; the launch traced here: 41 us
  waiting for transfers between devices  17.5 us (42%)
  starting transfers between devices  15.3 us (37%)
  Pallas kernels  4.64 us (11%)
  local copies, waits for them, and re-layouts  2.87 us (7%)
  between operations  0.69 us (2%)
    ppermute x20, waiting for transfers between devices, send(): return lax.ppermute(x, ('dp', 'rep'), pairs)  17.5 us
    ppermute x20, starting transfers between devices, send(): return lax.ppermute(x, ('dp', 'rep'), pairs)  15.3 us
    pallas_call x1, Pallas kernels, local(): pl.pallas_call(functools.partial(kernel, dp, rep, 3.0 / math.sqrt(width))...  4.64 us
    unnamed x6, local copies, waits for them, and re-layouts  1.9 us
    dynamic_slice x1, local copies, waits for them, and re-layouts, local(): own = lax.dynamic_slice_in_dim(head, core * half, half, axis=1)  0.97 us
  transfers between devices with their start and end apart: 20, of which 8 were waited for; matrix products, arithmetic and copies ran while one was open for 0% of the time, Pallas kernels for 0%

profile of v1, /device:TPU:0, one launch (start us, length us, event | category | flops | bytes accessed | tf_op | source)
XLA Modules:
  0.0 41.0 jit_solution(11601473835463495419)
XLA Ops:
  0.6 0.0 copy-start
  0.6 1.0 %constant_dynamic-slice_fusion = bf16[128,512]{1,0:T(8,128)(2,1)S(1)} fusion(bf16[128,1024]{1,0:T(8,128)(2,1)} %refs_0_.1, s32[]{:T(128)S(6)} %select_n.3), kind=kLoop, calls=%fused_computation | loop fusion | bytes 262148 | tf_op jit(solution)/shard_map/dynamic_slice | solution.py:100
  1.6 5.1 %collective-permute-start.5 = (bf16[128,512]{1,0:T(8,128)(2,1)S(1)}, bf16[128,512]{1,0:T(8,128)(2,1)S(1)}, u32[]{:S(2)}, u32[]{:S(2)}) collective-permute-start(bf16[128,512]{1,0:T(8,128)(2,1)S(1)} %constant_dynamic-slice_fusion), channel_id=1, source_target_pairs={{0,24},{1,25},{2,26},{3,27},{4,28},{5,29},{6,30},{7,31},{8,16},{9,... | collective-permute-start | bytes 393224 | tf_op jit(solution)/shard_map/ppermute | solution.py:94
  6.7 0.0 collective-permute-start.3
  6.7 0.6 %collective-permute-start.1 = (bf16[128,512]{1,0:T(8,128)(2,1)S(1)}, bf16[128,512]{1,0:T(8,128)(2,1)S(1)}, u32[]{:S(2)}, u32[]{:S(2)}) collective-permute-start(bf16[128,512]{1,0:T(8,128)(2,1)S(1)} %constant_dynamic-slice_fusion), channel_id=1, source_target_pairs={{0,8},{1,9},{2,10},{3,11},{4,12},{5,13},{6,14},{7,15},{8,0},{9,1},... | collective-permute-start | bytes 393224 | tf_op jit(solution)/shard_map/ppermute | solution.py:94
  7.4 1.7 %collective-permute-start = (bf16[128,512]{1,0:T(8,128)(2,1)S(1)}, bf16[128,512]{1,0:T(8,128)(2,1)S(1)}, u32[]{:S(2)}, u32[]{:S(2)}) collective-permute-start(bf16[128,512]{1,0:T(8,128)(2,1)S(1)} %constant_dynamic-slice_fusion), channel_id=1, source_target_pairs={{0,4},{1,5},{2,6},{3,7},{4,0},{5,1},{6,2},{7,3},{8,12},{9,13},{10,... | collective-permute-start | bytes 393224 | tf_op jit(solution)/shard_map/ppermute | solution.py:94
  9.0 2.1 %collective-permute-done.5.refs_6_ = bf16[128,512]{1,0:T(8,128)(2,1)S(1)} collective-permute-done((bf16[128,512]{1,0:T(8,128)(2,1)S(1)}, bf16[128,512]{1,0:T(8,128)(2,1)S(1)}, u32[]{:S(2)}, u32[]{:S(2)}) %collective-permute-start.5) | collective-permute-done | bytes 131104 | tf_op jit(solution)/shard_map/ppermute | solution.py:94
  11.2 0.0 collective-permute-start.12
  11.2 1.7 %collective-permute-start.6 = (bf16[128,512]{1,0:T(8,128)(2,1)S(1)}, bf16[128,512]{1,0:T(8,128)(2,1)S(1)}, u32[]{:S(2)}, u32[]{:S(2)}) collective-permute-start(bf16[128,512]{1,0:T(8,128)(2,1)S(1)} %collective-permute-done.5.refs_6_), channel_id=1, source_target_pairs={{0,4},{1,5},{2,6},{3,7},{4,0},{5,1},{6,2},{7,3},{8,12},{9,13},{10,... | collective-permute-start | bytes 393224 | tf_op jit(solution)/shard_map/ppermute | solution.py:94
  12.9 4.9 %collective-permute-done.3.refs_4_ = bf16[128,512]{1,0:T(8,128)(2,1)S(1)} collective-permute-done((bf16[128,512]{1,0:T(8,128)(2,1)S(1)}, bf16[128,512]{1,0:T(8,128)(2,1)S(1)}, u32[]{:S(2)}, u32[]{:S(2)}) %collective-permute-start.3) | collective-permute-done | bytes 131104 | tf_op jit(solution)/shard_map/ppermute | solution.py:94
  17.8 0.0 collective-permute-start.10
  17.8 0.0 collective-permute-done.1.refs_2_
  17.8 1.5 %collective-permute-start.18 = (bf16[128,1024]{1,0:T(8,128)(2,1)}, bf16[128,1024]{1,0:T(8,128)(2,1)S(1)}, u32[]{:S(2)}, u32[]{:S(2)}) collective-permute-start(bf16[128,1024]{1,0:T(8,128)(2,1)} %refs_19_.1), channel_id=1, source_target_pairs={{0,2},{1,3},{2,0},{3,1},{4,6},{5,7},{6,4},{7,5},{8,10},{9,11},{10,... | collective-permute-start | bytes 786440 | tf_op jit(solution)/shard_map/ppermute | solution.py:94
  19.3 0.0 collective-permute-done.refs_1_
  19.3 1.5 %collective-permute-start.4 = (bf16[128,512]{1,0:T(8,128)(2,1)S(1)}, bf16[128,512]{1,0:T(8,128)(2,1)S(1)}, u32[]{:S(2)}, u32[]{:S(2)}) collective-permute-start(bf16[128,512]{1,0:T(8,128)(2,1)S(1)} %collective-permute-done.3.refs_4_), channel_id=1, source_target_pairs={{0,4},{1,5},{2,6},{3,7},{4,0},{5,1},{6,2},{7,3},{8,12},{9,13},{10,... | collective-permute-start | bytes 393224 | tf_op jit(solution)/shard_map/ppermute | solution.py:94
  20.8 0.0 collective-permute-done.12.refs_13_
  20.8 0.0 collective-permute-start.8
  20.8 0.0 collective-permute-done.6.refs_7_
  20.8 0.6 %collective-permute-start.15 = (bf16[128,1024]{1,0:T(8,128)(2,1)}, bf16[128,1024]{1,0:T(8,128)(2,1)S(1)}, u32[]{:S(2)}, u32[]{:S(2)}) collective-permute-start(bf16[128,1024]{1,0:T(8,128)(2,1)} %refs_15_.1), channel_id=1, source_target_pairs={{0,2},{1,3},{2,0},{3,1},{4,6},{5,7},{6,4},{7,5},{8,10},{9,11},{10,... | collective-permute-start | bytes 786440 | tf_op jit(solution)/shard_map/ppermute | solution.py:94
  21.4 0.0 collective-permute-done.10.refs_11_
  21.4 0.5 %collective-permute-start.2 = (bf16[128,512]{1,0:T(8,128)(2,1)S(1)}, bf16[128,512]{1,0:T(8,128)(2,1)S(1)}, u32[]{:S(2)}, u32[]{:S(2)}) collective-permute-start(bf16[128,512]{1,0:T(8,128)(2,1)S(1)} %collective-permute-done.1.refs_2_), channel_id=1, source_target_pairs={{0,4},{1,5},{2,6},{3,7},{4,0},{5,1},{6,2},{7,3},{8,12},{9,13},{10,... | collective-permute-start | bytes 393224 | tf_op jit(solution)/shard_map/ppermute | solution.py:94
  22.0 3.7 %collective-permute-done.4.refs_5_ = bf16[128,512]{1,0:T(8,128)(2,1)S(1)} collective-permute-done((bf16[128,512]{1,0:T(8,128)(2,1)S(1)}, bf16[128,512]{1,0:T(8,128)(2,1)S(1)}, u32[]{:S(2)}, u32[]{:S(2)}) %collective-permute-start.4) | collective-permute-done | bytes 131104 | tf_op jit(solution)/shard_map/ppermute | solution.py:94
  25.6 0.0 collective-permute-start.17
  25.6 0.0 collective-permute-done.8.refs_9_
  25.7 0.5 %collective-permute-start.14 = (bf16[128,1024]{1,0:T(8,128)(2,1)}, bf16[128,1024]{1,0:T(8,128)(2,1)S(1)}, u32[]{:S(2)}, u32[]{:S(2)}) collective-permute-start(bf16[128,1024]{1,0:T(8,128)(2,1)} %refs_15_.1), channel_id=1, source_target_pairs={{0,1},{1,0},{2,3},{3,2},{4,5},{5,4},{6,7},{7,6},{8,9},{9,8},{10,11... | collective-permute-start | bytes 786440 | tf_op jit(solution)/shard_map/ppermute | solution.py:94
  26.2 1.6 %collective-permute-done.2.refs_3_ = bf16[128,512]{1,0:T(8,128)(2,1)S(1)} collective-permute-done((bf16[128,512]{1,0:T(8,128)(2,1)S(1)}, bf16[128,512]{1,0:T(8,128)(2,1)S(1)}, u32[]{:S(2)}, u32[]{:S(2)}) %collective-permute-start.2) | collective-permute-done | bytes 131104 | tf_op jit(solution)/shard_map/ppermute | solution.py:94
  27.8 0.0 collective-permute-start.7
  27.8 0.0 collective-permute-done.18.refs_21_
  27.8 0.5 %collective-permute-start.19 = (bf16[128,1024]{1,0:T(8,128)(2,1)S(1)}, bf16[128,1024]{1,0:T(8,128)(2,1)S(1)}, u32[]{:S(2)}, u32[]{:S(2)}) collective-permute-start(bf16[128,1024]{1,0:T(8,128)(2,1)S(1)} %collective-permute-done.18.refs_21_), channel_id=1, source_target_pairs={{0,1},{1,0},{2,3},{3,2},{4,5},{5,4},{6,7},{7,6},{8,9},{9,8},{10,11... | collective-permute-start | bytes 786440 | tf_op jit(solution)/shard_map/ppermute | solution.py:94
  28.3 4.1 %collective-permute-done.15.refs_17_ = bf16[128,1024]{1,0:T(8,128)(2,1)S(1)} collective-permute-done((bf16[128,1024]{1,0:T(8,128)(2,1)}, bf16[128,1024]{1,0:T(8,128)(2,1)S(1)}, u32[]{:S(2)}, u32[]{:S(2)}) %collective-permute-start.15) | collective-permute-done | bytes 262176 | tf_op jit(solution)/shard_map/ppermute | solution.py:94
  32.4 0.0 collective-permute-start.16
  32.4 0.0 collective-permute-done.7.refs_8_
  32.4 0.5 %collective-permute-start.13 = (bf16[128,512]{1,0:T(8,128)(2,1)S(1)}, bf16[128,512]{1,0:T(8,128)(2,1)S(1)}, u32[]{:S(2)}, u32[]{:S(2)}) collective-permute-start(bf16[128,512]{1,0:T(8,128)(2,1)S(1)} %collective-permute-done.6.refs_7_), channel_id=1, source_target_pairs={{0,1},{1,0},{2,3},{3,2},{4,5},{5,4},{6,7},{7,6},{8,9},{9,8},{10,11... | collective-permute-start | bytes 393224 | tf_op jit(solution)/shard_map/ppermute | solution.py:94
  32.9 0.0 collective-permute-done.17.refs_20_
  32.9 0.1 collective-permute-start.11
  33.0 0.0 collective-permute-done.14.refs_16_
  33.0 0.4 %collective-permute-start.9 = (bf16[128,512]{1,0:T(8,128)(2,1)S(1)}, bf16[128,512]{1,0:T(8,128)(2,1)S(1)}, u32[]{:S(2)}, u32[]{:S(2)}) collective-permute-start(bf16[128,512]{1,0:T(8,128)(2,1)S(1)} %collective-permute-done.2.refs_3_), channel_id=1, source_target_pairs={{0,1},{1,0},{2,3},{3,2},{4,5},{5,4},{6,7},{7,6},{8,9},{9,8},{10,11... | collective-permute-start | bytes 393224 | tf_op jit(solution)/shard_map/ppermute | solution.py:94
  33.4 0.7 %collective-permute-done.13.refs_14_ = bf16[128,512]{1,0:T(8,128)(2,1)S(1)} collective-permute-done((bf16[128,512]{1,0:T(8,128)(2,1)S(1)}, bf16[128,512]{1,0:T(8,128)(2,1)S(1)}, u32[]{:S(2)}, u32[]{:S(2)}) %collective-permute-start.13) | collective-permute-done | bytes 131104 | tf_op jit(solution)/shard_map/ppermute | solution.py:94
  34.1 0.2 collective-permute-done.11.refs_12_
  34.3 0.2 collective-permute-done.9.refs_10_
  34.5 0.0 collective-permute-done.19.refs_22_
  34.5 0.0 collective-permute-done.16.refs_18_
  34.5 0.0 copy-done
  34.5 0.0 copy-start.1
  34.5 0.9 %copy-done.1 = bf16[128,1024]{1,0:T(8,128)(2,1)S(1)} copy-done((bf16[128,1024]{1,0:T(8,128)(2,1)S(1)}, bf16[128,1024]{1,0:T(8,128)(2,1)}, u32[]{:S(2)}) %copy-start.1) | copy-done | bytes 262168
  35.4 0.0 copy-start.2
  35.4 0.9 %copy-done.2 = bf16[128,1024]{1,0:T(8,128)(2,1)S(1)} copy-done((bf16[128,1024]{1,0:T(8,128)(2,1)S(1)}, bf16[128,1024]{1,0:T(8,128)(2,1)}, u32[]{:S(2)}) %copy-start.2) | copy-done | bytes 262168
  36.4 4.6 %group_softmax.1 = (f32[128]{0:T(128)}, bf16[128,1024]{1,0:T(8,128)(2,1)}, bf16[128,1024]{1,0:T(8,128)(2,1)}) custom-call(bf16[128,1024]{1,0:T(8,128)(2,1)S(1)} %copy-done, bf16[128,512]{1,0:T(8,128)(2,1)S(1)} %collective-permute-done.refs_1_, bf16[128,512]{1,0:T(8,128)(2,1)S(1)} %collective-permute-done.1.refs_2_, ...), custom_call_target="tpu_custom_call" | custom-call | tf_op jit(solution)/shard_map/group_softmax/pallas_call | solution.py:126
Async XLA Ops:
  0.6 33.8 %copy-start = (bf16[128,1024]{1,0:T(8,128)(2,1)S(1)}, bf16[128,1024]{1,0:T(8,128)(2,1)}, u32[]{:S(2)}) copy-start(bf16[128,1024]{1,0:T(8,128)(2,1)} %refs_0_.1) | copy-start | bytes 786436
  1.6 9.5 %collective-permute-start.5 = (bf16[128,512]{1,0:T(8,128)(2,1)S(1)}, bf16[128,512]{1,0:T(8,128)(2,1)S(1)}, u32[]{:S(2)}, u32[]{:S(2)}) collective-permute-start(bf16[128,512]{1,0:T(8,128)(2,1)S(1)} %constant_dynamic-slice_fusion), channel_id=1, source_target_pairs={{0,24},{1,25},{2,26},{3,27},{4,28},{5,29},{6,30},{7,31},{8,16},{9,... | collective-permute-start | bytes 393224 | tf_op jit(solution)/shard_map/ppermute | solution.py:94
  6.7 11.1 %collective-permute-start.3 = (bf16[128,512]{1,0:T(8,128)(2,1)S(1)}, bf16[128,512]{1,0:T(8,128)(2,1)S(1)}, u32[]{:S(2)}, u32[]{:S(2)}) collective-permute-start(bf16[128,512]{1,0:T(8,128)(2,1)S(1)} %constant_dynamic-slice_fusion), channel_id=1, source_target_pairs={{0,16},{1,17},{2,18},{3,19},{4,20},{5,21},{6,22},{7,23},{8,24},{9,... | collective-permute-start | bytes 393224 | tf_op jit(solution)/shard_map/ppermute | solution.py:94
  6.7 11.1 %collective-permute-start.1 = (bf16[128,512]{1,0:T(8,128)(2,1)S(1)}, bf16[128,512]{1,0:T(8,128)(2,1)S(1)}, u32[]{:S(2)}, u32[]{:S(2)}) collective-permute-start(bf16[128,512]{1,0:T(8,128)(2,1)S(1)} %constant_dynamic-slice_fusion), channel_id=1, source_target_pairs={{0,8},{1,9},{2,10},{3,11},{4,12},{5,13},{6,14},{7,15},{8,0},{9,1},... | collective-permute-start | bytes 393224 | tf_op jit(solution)/shard_map/ppermute | solution.py:94
  7.4 11.9 %collective-permute-start = (bf16[128,512]{1,0:T(8,128)(2,1)S(1)}, bf16[128,512]{1,0:T(8,128)(2,1)S(1)}, u32[]{:S(2)}, u32[]{:S(2)}) collective-permute-start(bf16[128,512]{1,0:T(8,128)(2,1)S(1)} %constant_dynamic-slice_fusion), channel_id=1, source_target_pairs={{0,4},{1,5},{2,6},{3,7},{4,0},{5,1},{6,2},{7,3},{8,12},{9,13},{10,... | collective-permute-start | bytes 393224 | tf_op jit(solution)/shard_map/ppermute | solution.py:94
  11.2 9.7 %collective-permute-start.12 = (bf16[128,512]{1,0:T(8,128)(2,1)S(1)}, bf16[128,512]{1,0:T(8,128)(2,1)S(1)}, u32[]{:S(2)}, u32[]{:S(2)}) collective-permute-start(bf16[128,512]{1,0:T(8,128)(2,1)S(1)} %collective-permute-done.5.refs_6_), channel_id=1, source_target_pairs={{0,1},{1,0},{2,3},{3,2},{4,5},{5,4},{6,7},{7,6},{8,9},{9,8},{10,11... | collective-permute-start | bytes 393224 | tf_op jit(solution)/shard_map/ppermute | solution.py:94
  11.2 9.7 %collective-permute-start.6 = (bf16[128,512]{1,0:T(8,128)(2,1)S(1)}, bf16[128,512]{1,0:T(8,128)(2,1)S(1)}, u32[]{:S(2)}, u32[]{:S(2)}) collective-permute-start(bf16[128,512]{1,0:T(8,128)(2,1)S(1)} %collective-permute-done.5.refs_6_), channel_id=1, source_target_pairs={{0,4},{1,5},{2,6},{3,7},{4,0},{5,1},{6,2},{7,3},{8,12},{9,13},{10,... | collective-permute-start | bytes 393224 | tf_op jit(solution)/shard_map/ppermute | solution.py:94
  17.8 3.6 %collective-permute-start.10 = (bf16[128,512]{1,0:T(8,128)(2,1)S(1)}, bf16[128,512]{1,0:T(8,128)(2,1)S(1)}, u32[]{:S(2)}, u32[]{:S(2)}) collective-permute-start(bf16[128,512]{1,0:T(8,128)(2,1)S(1)} %collective-permute-done.3.refs_4_), channel_id=1, source_target_pairs={{0,1},{1,0},{2,3},{3,2},{4,5},{5,4},{6,7},{7,6},{8,9},{9,8},{10,11... | collective-permute-start | bytes 393224 | tf_op jit(solution)/shard_map/ppermute | solution.py:94
  17.8 9.9 %collective-permute-start.18 = (bf16[128,1024]{1,0:T(8,128)(2,1)}, bf16[128,1024]{1,0:T(8,128)(2,1)S(1)}, u32[]{:S(2)}, u32[]{:S(2)}) collective-permute-start(bf16[128,1024]{1,0:T(8,128)(2,1)} %refs_19_.1), channel_id=1, source_target_pairs={{0,2},{1,3},{2,0},{3,1},{4,6},{5,7},{6,4},{7,5},{8,10},{9,11},{10,... | collective-permute-start | bytes 786440 | tf_op jit(solution)/shard_map/ppermute | solution.py:94
  19.3 6.3 %collective-permute-start.4 = (bf16[128,512]{1,0:T(8,128)(2,1)S(1)}, bf16[128,512]{1,0:T(8,128)(2,1)S(1)}, u32[]{:S(2)}, u32[]{:S(2)}) collective-permute-start(bf16[128,512]{1,0:T(8,128)(2,1)S(1)} %collective-permute-done.3.refs_4_), channel_id=1, source_target_pairs={{0,4},{1,5},{2,6},{3,7},{4,0},{5,1},{6,2},{7,3},{8,12},{9,13},{10,... | collective-permute-start | bytes 393224 | tf_op jit(solution)/shard_map/ppermute | solution.py:94
  20.8 4.8 %collective-permute-start.8 = (bf16[128,512]{1,0:T(8,128)(2,1)S(1)}, bf16[128,512]{1,0:T(8,128)(2,1)S(1)}, u32[]{:S(2)}, u32[]{:S(2)}) collective-permute-start(bf16[128,512]{1,0:T(8,128)(2,1)S(1)} %collective-permute-done.1.refs_2_), channel_id=1, source_target_pairs={{0,1},{1,0},{2,3},{3,2},{4,5},{5,4},{6,7},{7,6},{8,9},{9,8},{10,11... | collective-permute-start | bytes 393224 | tf_op jit(solution)/shard_map/ppermute | solution.py:94
  20.8 11.5 %collective-permute-start.15 = (bf16[128,1024]{1,0:T(8,128)(2,1)}, bf16[128,1024]{1,0:T(8,128)(2,1)S(1)}, u32[]{:S(2)}, u32[]{:S(2)}) collective-permute-start(bf16[128,1024]{1,0:T(8,128)(2,1)} %refs_15_.1), channel_id=1, source_target_pairs={{0,2},{1,3},{2,0},{3,1},{4,6},{5,7},{6,4},{7,5},{8,10},{9,11},{10,... | collective-permute-start | bytes 786440 | tf_op jit(solution)/shard_map/ppermute | solution.py:94
  21.4 6.3 %collective-permute-start.2 = (bf16[128,512]{1,0:T(8,128)(2,1)S(1)}, bf16[128,512]{1,0:T(8,128)(2,1)S(1)}, u32[]{:S(2)}, u32[]{:S(2)}) collective-permute-start(bf16[128,512]{1,0:T(8,128)(2,1)S(1)} %collective-permute-done.1.refs_2_), channel_id=1, source_target_pairs={{0,4},{1,5},{2,6},{3,7},{4,0},{5,1},{6,2},{7,3},{8,12},{9,13},{10,... | collective-permute-start | bytes 393224 | tf_op jit(solution)/shard_map/ppermute | solution.py:94
  25.6 7.2 %collective-permute-start.17 = (bf16[128,1024]{1,0:T(8,128)(2,1)}, bf16[128,1024]{1,0:T(8,128)(2,1)S(1)}, u32[]{:S(2)}, u32[]{:S(2)}) collective-permute-start(bf16[128,1024]{1,0:T(8,128)(2,1)} %refs_19_.1), channel_id=1, source_target_pairs={{0,1},{1,0},{2,3},{3,2},{4,5},{5,4},{6,7},{7,6},{8,9},{9,8},{10,11... | collective-permute-start | bytes 786440 | tf_op jit(solution)/shard_map/ppermute | solution.py:94
  25.7 7.3 %collective-permute-start.14 = (bf16[128,1024]{1,0:T(8,128)(2,1)}, bf16[128,1024]{1,0:T(8,128)(2,1)S(1)}, u32[]{:S(2)}, u32[]{:S(2)}) collective-permute-start(bf16[128,1024]{1,0:T(8,128)(2,1)} %refs_15_.1), channel_id=1, source_target_pairs={{0,1},{1,0},{2,3},{3,2},{4,5},{5,4},{6,7},{7,6},{8,9},{9,8},{10,11... | collective-permute-start | bytes 786440 | tf_op jit(solution)/shard_map/ppermute | solution.py:94
  27.8 4.6 %collective-permute-start.7 = (bf16[128,512]{1,0:T(8,128)(2,1)S(1)}, bf16[128,512]{1,0:T(8,128)(2,1)S(1)}, u32[]{:S(2)}, u32[]{:S(2)}) collective-permute-start(bf16[128,512]{1,0:T(8,128)(2,1)S(1)} %collective-permute-done.refs_1_), channel_id=1, source_target_pairs={{0,1},{1,0},{2,3},{3,2},{4,5},{5,4},{6,7},{7,6},{8,9},{9,8},{10,11... | collective-permute-start | bytes 393224 | tf_op jit(solution)/shard_map/ppermute | solution.py:94
  27.8 6.7 %collective-permute-start.19 = (bf16[128,1024]{1,0:T(8,128)(2,1)S(1)}, bf16[128,1024]{1,0:T(8,128)(2,1)S(1)}, u32[]{:S(2)}, u32[]{:S(2)}) collective-permute-start(bf16[128,1024]{1,0:T(8,128)(2,1)S(1)} %collective-permute-done.18.refs_21_), channel_id=1, source_target_pairs={{0,1},{1,0},{2,3},{3,2},{4,5},{5,4},{6,7},{7,6},{8,9},{9,8},{10,11... | collective-permute-start | bytes 786440 | tf_op jit(solution)/shard_map/ppermute | solution.py:94
  32.4 2.1 %collective-permute-start.16 = (bf16[128,1024]{1,0:T(8,128)(2,1)S(1)}, bf16[128,1024]{1,0:T(8,128)(2,1)S(1)}, u32[]{:S(2)}, u32[]{:S(2)}) collective-permute-start(bf16[128,1024]{1,0:T(8,128)(2,1)S(1)} %collective-permute-done.15.refs_17_), channel_id=1, source_target_pairs={{0,1},{1,0},{2,3},{3,2},{4,5},{5,4},{6,7},{7,6},{8,9},{9,8},{10,11... | collective-permute-start | bytes 786440 | tf_op jit(solution)/shard_map/ppermute | solution.py:94
  32.4 1.7 %collective-permute-start.13 = (bf16[128,512]{1,0:T(8,128)(2,1)S(1)}, bf16[128,512]{1,0:T(8,128)(2,1)S(1)}, u32[]{:S(2)}, u32[]{:S(2)}) collective-permute-start(bf16[128,512]{1,0:T(8,128)(2,1)S(1)} %collective-permute-done.6.refs_7_), channel_id=1, source_target_pairs={{0,1},{1,0},{2,3},{3,2},{4,5},{5,4},{6,7},{7,6},{8,9},{9,8},{10,11... | collective-permute-start | bytes 393224 | tf_op jit(solution)/shard_map/ppermute | solution.py:94
  32.9 1.4 %collective-permute-start.11 = (bf16[128,512]{1,0:T(8,128)(2,1)S(1)}, bf16[128,512]{1,0:T(8,128)(2,1)S(1)}, u32[]{:S(2)}, u32[]{:S(2)}) collective-permute-start(bf16[128,512]{1,0:T(8,128)(2,1)S(1)} %collective-permute-done.4.refs_5_), channel_id=1, source_target_pairs={{0,1},{1,0},{2,3},{3,2},{4,5},{5,4},{6,7},{7,6},{8,9},{9,8},{10,11... | collective-permute-start | bytes 393224 | tf_op jit(solution)/shard_map/ppermute | solution.py:94
  33.0 1.5 %collective-permute-start.9 = (bf16[128,512]{1,0:T(8,128)(2,1)S(1)}, bf16[128,512]{1,0:T(8,128)(2,1)S(1)}, u32[]{:S(2)}, u32[]{:S(2)}) collective-permute-start(bf16[128,512]{1,0:T(8,128)(2,1)S(1)} %collective-permute-done.2.refs_3_), channel_id=1, source_target_pairs={{0,1},{1,0},{2,3},{3,2},{4,5},{5,4},{6,7},{7,6},{8,9},{9,8},{10,11... | collective-permute-start | bytes 393224 | tf_op jit(solution)/shard_map/ppermute | solution.py:94
  34.5 1.0 %copy-start.1 = (bf16[128,1024]{1,0:T(8,128)(2,1)S(1)}, bf16[128,1024]{1,0:T(8,128)(2,1)}, u32[]{:S(2)}) copy-start(bf16[128,1024]{1,0:T(8,128)(2,1)} %refs_15_.1) | copy-start | bytes 786436
  35.4 0.9 %copy-start.2 = (bf16[128,1024]{1,0:T(8,128)(2,1)S(1)}, bf16[128,1024]{1,0:T(8,128)(2,1)}, u32[]{:S(2)}) copy-start(bf16[128,1024]{1,0:T(8,128)(2,1)} %refs_19_.1) | copy-start | bytes 786436

commit v2 on v1

--- a/solution.py
+++ b/solution.py
@@ -16,17 +16,16 @@
     return lax.dot_general(left, right, contract, preferred_element_type=jnp.float32)
 
 
-def kernel(dp, rep, scale, *refs):
+def kernel(dp, rep, scale, slots, *refs):
     head_ref, refs = refs[0], refs[1:]
-    mine_refs, refs = refs[: dp - 1], refs[dp - 1 :]
-    theirs_refs, refs = refs[: dp - 1], refs[dp - 1 :]
+    pieces, refs = refs[: 2 * len(slots)], refs[2 * len(slots) :]
     entity_refs, refs = refs[:rep], refs[rep:]
     mention_refs, refs = refs[:rep], refs[rep:]
     loss_ref, mention_grad_ref, state_grad_ref = refs[:3]
     head, entities, mentions, projected, sems = refs[3:]
 
     rows = entity_refs[0].shape[0]
-    depth, half = head_ref.shape[0], mine_refs[0].shape[1]
+    depth = head_ref.shape[0]
     me, core = lax.axis_index("dp"), lax.rem(lax.axis_index("rep"), 2)
 
     copies = []
@@ -36,16 +35,23 @@
         copy.start()
         copies.append(copy)
 
-    def place(mask, column):
+    def place(mask):
         at = pl.multiple_of(jnp.bitwise_xor(me, mask) * depth, depth)
-        return head.at[pl.ds(at, depth), pl.ds(pl.multiple_of(column * half, half), half)]
+        return head.at[pl.ds(at, depth)]
 
     for i in range(rep):
         fetch(entity_refs[i], entities.at[pl.ds(i * rows, rows)])
-    fetch(head_ref, head.at[pl.ds(pl.multiple_of(me * depth, depth), depth)])
-    for mask in range(1, dp):
-        fetch(mine_refs[mask - 1], place(mask, core))
-        fetch(theirs_refs[mask - 1], place(mask, 1 - core))
+    fetch(head_ref, place(0))
+    for i, (_, _, masks) in enumerate(slots):
+        near, other = pieces[2 * i : 2 * i + 2]
+        if masks[1] is None:
+            copy = pltpu.make_async_copy(near, place(masks[0]), sems.at[len(copies)])
+            pl.when(core == 0)(copy.start)
+            pl.when(core == 1)(pltpu.make_async_copy(other, place(masks[0]), sems.at[len(copies)]).start)
+            copies.append(copy)
+        else:
+            fetch(near, place(jnp.where(core == 0, *masks)))
+            fetch(other, place(jnp.where(core == 0, *masks[::-1])))
     ready = len(copies)
     for i in range(rep):
         fetch(mention_refs[i], mentions.at[pl.ds(i * rows, rows)])
@@ -84,47 +90,63 @@
     state_grad_ref[...] = dot(proj_grad, head[...], LAST).astype(jnp.bfloat16)
 
 
+def plan(dp):
+    children = {mask: [] for mask in range(dp)}
+    for mask in range(1, dp):
+        step = mask & -mask
+        children[0 if mask in (step, dp - 1) else mask ^ step].append(mask)
+    first = sorted(children[0], key=lambda m: (-len(children[m]), -m))
+    slots = [(-1, masks, masks) for masks in zip(first[::2], first[1::2] + [None] * (len(first) % 2))]
+    for i, (_, _, held) in enumerate(slots):
+        lists = [[] if m is None else children[m] for m in held]
+        for j in range(max(map(len, lists))):
+            masks = tuple(own[j] if j < len(own) else None for own in lists)
+            steps = tuple(None if m is None else m ^ h for m, h in zip(masks, held))
+            slots.append((i, steps, masks))
+    return slots
+
+
 def solution(mesh):
     dp, rep = mesh.shape["dp"], mesh.shape["rep"]
 
-    def send(x, over_dp, over_rep):
+    slots = plan(dp)
+
+    def send(x, over_dp, over_rep=0):
         pairs = [
-            (d * rep + r, (d ^ over_dp) * rep + (r ^ over_rep)) for d in range(dp) for r in range(rep)
+            (d * rep + r, (d ^ over_dp[r % 2]) * rep + (r ^ over_rep))
+            for d in range(dp)
+            for r in range(rep)
+            if over_dp[r % 2] is not None
         ]
         return lax.ppermute(x, ("dp", "rep"), pairs)
 
+    def after(x, done):
+        return lax.optimization_barrier((x, done))[0]
+
     def local(mentions, entity_states, head):
         rows, width = mentions.shape
-        half = width // 2
-        core = lax.rem(lax.axis_index("rep"), 2)
-        own = lax.dynamic_slice_in_dim(head, core * half, half, axis=1)
-
-        mine = {}
-        for mask in range(2, dp, 2):
-            mine[mask] = send(own, mask, 0)
-        mine[1] = send(own, 1, 0)
         entities, held = {0: entity_states}, {0: mentions}
         for store in (entities, held):
             for mask in range(2, rep, 2):
-                store[mask] = send(store[0], 0, mask)
-            for mask in range(0, rep, 2):
-                store[mask + 1] = send(store[mask], 0, 1)
-        for mask in range(2, dp, 2):
-            mine[mask + 1] = send(mine[mask], 1, 0)
-        theirs = {mask: send(mine[mask], 0, 1) for mask in range(1, dp)}
+                store[mask] = send(store[0], (0, 0), mask)
+        entities[1] = send(entities[0], (0, 0), 1)
+        pieces = []
+        for i, (source, steps, masks) in enumerate(slots):
+            start = head if i == 0 else after(head, entities[1])
+            near = send(start if source < 0 else pieces[2 * source], steps)
+            pieces += [near, send(near, [None if m is None else 0 for m in masks], 1)]
+        held[1] = send(after(held[0], pieces[0]), (0, 0), 1)
+        for store in (entities, held):
+            for mask in range(2, rep, 2):
+                store[mask + 1] = send(after(store[mask], pieces[0]), (0, 0), 1)
 
-        operands = (
-            [head]
-            + [mine[i] for i in range(1, dp)]
-            + [theirs[i] for i in range(1, dp)]
-            + [entities[i] for i in range(rep)]
-            + [held[i] for i in range(rep)]
-        )
+        head, entities[0], held[0] = (pltpu.with_memory_space_constraint(x, pltpu.HBM) for x in (head, entities[0], held[0]))
+        operands = [head] + pieces + [entities[i] for i in range(rep)] + [held[i] for i in range(rep)]
         group = rep * rows
         anywhere = pl.BlockSpec(memory_space=pl.ANY)
         vmem = pl.BlockSpec(memory_space=pltpu.VMEM)
         return pl.pallas_call(
-            functools.partial(kernel, dp, rep, 3.0 / math.sqrt(width)),
+            functools.partial(kernel, dp, rep, 3.0 / math.sqrt(width), slots),
             out_shape=(
                 jax.ShapeDtypeStruct((rows,), jnp.float32),
                 jax.ShapeDtypeStruct((rows, width), jnp.bfloat16),

time: 41.2 us -> 32 us (0.78)
  waiting for transfers between devices: 17.5 us -> 9.61 us
  local copies, waits for them, and re-layouts: 2.87 us -> 0 us
  starting transfers between devices: 15.3 us -> 16.3 us
  Pallas kernels: 4.64 us -> 5.24 us
    ppermute x20 -> x14, waiting for transfers between devices: 17.5 us -> 9.61 us  [send(): return lax.ppermute(x, ('dp', 'rep'), pairs)]
    unnamed x6 -> x0, local copies, waits for them, and re-layouts: 1.9 us -> none
    ppermute x20 -> x14, starting transfers between devices: 15.3 us -> 16.3 us  [send(): return lax.ppermute(x, ('dp', 'rep'), pairs)]
    dynamic_slice x1 -> x0, local copies, waits for them, and re-layouts: 0.97 us -> none  [local(): own = lax.dynamic_slice_in_dim(head, core * half, half, axis=1)]
    pallas_call x1, Pallas kernels: 4.64 us -> 5.24 us  [local(): pl.pallas_call(functools.partial(kernel, dp, rep, 3.0 / math.sqrt(width),...]
  transfers between devices with their start and end apart: 20 -> 14, of which waited for: 8 -> 6; matrix products, arithmetic and copies ran while one was open for 0% -> 0% of each run, Pallas kernels for 0% -> 0%
where the time goes in v2:
time: 32 us; the launch traced here: 31.8 us
  starting transfers between devices  16.3 us (51%)
  waiting for transfers between devices  9.61 us (30%)
  Pallas kernels  5.24 us (16%)
  between operations  0.68 us (2%)
    ppermute x14, starting transfers between devices, send(): return lax.ppermute(x, ('dp', 'rep'), pairs)  16.3 us
    ppermute x14, waiting for transfers between devices, send(): return lax.ppermute(x, ('dp', 'rep'), pairs)  9.61 us
    pallas_call x1, Pallas kernels, local(): pl.pallas_call(functools.partial(kernel, dp, rep, 3.0 / math.sqrt(width),...  5.24 us
  transfers between devices with their start and end apart: 14, of which 6 were waited for; matrix products, arithmetic and copies ran while one was open for 0% of the time, Pallas kernels for 0%

profile of v2, /device:TPU:0, one launch (start us, length us, event | category | flops | bytes accessed | tf_op | source)
XLA Modules:
  0.0 31.8 jit_solution(6259108855399276861)
XLA Ops:
  0.6 0.5 %collective-permute-start.2 = (bf16[128,1024]{1,0:T(8,128)(2,1)}, bf16[128,1024]{1,0:T(8,128)(2,1)S(1)}, u32[]{:S(2)}, u32[]{:S(2)}) collective-permute-start(bf16[128,1024]{1,0:T(8,128)(2,1)} %refs_9_.1), channel_id=1, source_target_pairs={{0,1},{1,0},{2,3},{3,2},{4,5},{5,4},{6,7},{7,6},{8,9},{9,8},{10,11... | collective-permute-start | bytes 786440 | tf_op jit(solution)/shard_map/ppermute | solution.py:121
  1.1 3.7 %collective-permute-start = (bf16[128,1024]{1,0:T(8,128)(2,1)}, bf16[128,1024]{1,0:T(8,128)(2,1)S(1)}, u32[]{:S(2)}, u32[]{:S(2)}) collective-permute-start(bf16[128,1024]{1,0:T(8,128)(2,1)} %refs_0_.1), channel_id=1, source_target_pairs={{0,16},{1,9},{2,18},{3,11},{4,20},{5,13},{6,22},{7,15},{8,24},{9,1... | collective-permute-start | bytes 786440 | tf_op jit(solution)/shard_map/ppermute | solution.py:121
  4.8 1.5 %collective-permute-start.9 = (bf16[128,1024]{1,0:T(8,128)(2,1)}, bf16[128,1024]{1,0:T(8,128)(2,1)S(1)}, u32[]{:S(2)}, u32[]{:S(2)}) collective-permute-start(bf16[128,1024]{1,0:T(8,128)(2,1)} %refs_9_.1), channel_id=1, source_target_pairs={{0,2},{1,3},{2,0},{3,1},{4,6},{5,7},{6,4},{7,5},{8,10},{9,11},{10,... | collective-permute-start | bytes 786440 | tf_op jit(solution)/shard_map/ppermute | solution.py:121
  6.3 0.5 %collective-permute-start.12 = (bf16[128,1024]{1,0:T(8,128)(2,1)}, bf16[128,1024]{1,0:T(8,128)(2,1)S(1)}, u32[]{:S(2)}, u32[]{:S(2)}) collective-permute-start(bf16[128,1024]{1,0:T(8,128)(2,1)} %refs_13_.1), channel_id=1, source_target_pairs={{0,2},{1,3},{2,0},{3,1},{4,6},{5,7},{6,4},{7,5},{8,10},{9,11},{10,... | collective-permute-start | bytes 786440 | tf_op jit(solution)/shard_map/ppermute | solution.py:121
  6.8 0.0 collective-permute-done.2.refs_10_
  6.8 2.3 %collective-permute-start.3 = (bf16[128,1024]{1,0:T(8,128)(2,1)}, bf16[128,1024]{1,0:T(8,128)(2,1)S(1)}, u32[]{:S(2)}, u32[]{:S(2)}) collective-permute-start(bf16[128,1024]{1,0:T(8,128)(2,1)} %refs_0_.1), channel_id=1, source_target_pairs={{0,28},{1,5},{2,30},{3,7},{4,24},{5,1},{6,26},{7,3},{8,20},{9,13},... | collective-permute-start | bytes 786440 | tf_op jit(solution)/shard_map/ppermute | solution.py:121
  9.1 1.9 %collective-permute-done.refs_1_ = bf16[128,1024]{1,0:T(8,128)(2,1)S(1)} collective-permute-done((bf16[128,1024]{1,0:T(8,128)(2,1)}, bf16[128,1024]{1,0:T(8,128)(2,1)S(1)}, u32[]{:S(2)}, u32[]{:S(2)}) %collective-permute-start) | collective-permute-done | bytes 262176 | tf_op jit(solution)/shard_map/ppermute | solution.py:121
  11.0 3.3 %collective-permute-done.9.refs_11_ = bf16[128,1024]{1,0:T(8,128)(2,1)S(1)} collective-permute-done((bf16[128,1024]{1,0:T(8,128)(2,1)}, bf16[128,1024]{1,0:T(8,128)(2,1)S(1)}, u32[]{:S(2)}, u32[]{:S(2)}) %collective-permute-start.9) | collective-permute-done | bytes 262176 | tf_op jit(solution)/shard_map/ppermute | solution.py:121
  14.3 0.0 collective-permute-start.10
  14.3 0.5 %collective-permute-start.11 = (bf16[128,1024]{1,0:T(8,128)(2,1)}, bf16[128,1024]{1,0:T(8,128)(2,1)S(1)}, u32[]{:S(2)}, u32[]{:S(2)}) collective-permute-start(bf16[128,1024]{1,0:T(8,128)(2,1)} %refs_13_.1), channel_id=1, source_target_pairs={{0,1},{1,0},{2,3},{3,2},{4,5},{5,4},{6,7},{7,6},{8,9},{9,8},{10,11... | collective-permute-start | bytes 786440 | tf_op jit(solution)/shard_map/ppermute | solution.py:121
  14.8 3.8 %collective-permute-start.7 = (bf16[128,1024]{1,0:T(8,128)(2,1)S(1)}, bf16[128,1024]{1,0:T(8,128)(2,1)S(1)}, u32[]{:S(2)}, u32[]{:S(2)}) collective-permute-start(bf16[128,1024]{1,0:T(8,128)(2,1)S(1)} %collective-permute-done.refs_1_), channel_id=1, source_target_pairs={{0,8},{2,10},{4,12},{6,14},{8,0},{10,2},{12,4},{14,6},{16,24},{18,... | collective-permute-start | bytes 786440 | tf_op jit(solution)/shard_map/ppermute | solution.py:121
  18.6 0.0 collective-permute-done.12.refs_15_
  18.6 1.6 %collective-permute-start.5 = (bf16[128,1024]{1,0:T(8,128)(2,1)S(1)}, bf16[128,1024]{1,0:T(8,128)(2,1)S(1)}, u32[]{:S(2)}, u32[]{:S(2)}) collective-permute-start(bf16[128,1024]{1,0:T(8,128)(2,1)S(1)} %collective-permute-done.refs_1_), channel_id=1, source_target_pairs={{0,4},{1,5},{2,6},{3,7},{4,0},{5,1},{6,2},{7,3},{8,12},{9,13},{10,... | collective-permute-start | bytes 786440 | tf_op jit(solution)/shard_map/ppermute | solution.py:121
  20.2 0.0 collective-permute-done.3.refs_3_
  20.2 0.0 collective-permute-start.13
  20.2 0.0 collective-permute-done.10.refs_12_
  20.2 0.5 %collective-permute-start.1 = (bf16[128,1024]{1,0:T(8,128)(2,1)S(1)}, bf16[128,1024]{1,0:T(8,128)(2,1)S(1)}, u32[]{:S(2)}, u32[]{:S(2)}) collective-permute-start(bf16[128,1024]{1,0:T(8,128)(2,1)S(1)} %collective-permute-done.refs_1_), channel_id=1, source_target_pairs={{0,1},{1,0},{2,3},{3,2},{4,5},{5,4},{6,7},{7,6},{8,9},{9,8},{10,11... | collective-permute-start | bytes 786440 | tf_op jit(solution)/shard_map/ppermute | solution.py:121
  20.7 0.0 collective-permute-done.11.refs_14_
  20.7 0.1 collective-permute-start.4
  20.8 2.2 %collective-permute-done.7.refs_7_ = bf16[128,1024]{1,0:T(8,128)(2,1)S(1)} collective-permute-done((bf16[128,1024]{1,0:T(8,128)(2,1)S(1)}, bf16[128,1024]{1,0:T(8,128)(2,1)S(1)}, u32[]{:S(2)}, u32[]{:S(2)}) %collective-permute-start.7) | collective-permute-done | bytes 262176 | tf_op jit(solution)/shard_map/ppermute | solution.py:121
  23.0 1.3 %collective-permute-start.8 = (bf16[128,1024]{1,0:T(8,128)(2,1)S(1)}, bf16[128,1024]{1,0:T(8,128)(2,1)S(1)}, u32[]{:S(2)}, u32[]{:S(2)}) collective-permute-start(bf16[128,1024]{1,0:T(8,128)(2,1)S(1)} %collective-permute-done.7.refs_7_), channel_id=1, source_target_pairs={{0,1},{2,3},{4,5},{6,7},{8,9},{10,11},{12,13},{14,15},{16,17},{18,... | collective-permute-start | bytes 786440 | tf_op jit(solution)/shard_map/ppermute | solution.py:121
  24.3 0.7 %collective-permute-done.5.refs_5_ = bf16[128,1024]{1,0:T(8,128)(2,1)S(1)} collective-permute-done((bf16[128,1024]{1,0:T(8,128)(2,1)S(1)}, bf16[128,1024]{1,0:T(8,128)(2,1)S(1)}, u32[]{:S(2)}, u32[]{:S(2)}) %collective-permute-start.5) | collective-permute-done | bytes 262176 | tf_op jit(solution)/shard_map/ppermute | solution.py:121
  25.1 0.0 collective-permute-start.6
  25.1 0.0 collective-permute-done.13.refs_16_
  25.1 0.0 collective-permute-done.1.refs_2_
  25.1 0.0 collective-permute-done.4.refs_4_
  25.1 0.4 %collective-permute-done.8.refs_8_ = bf16[128,1024]{1,0:T(8,128)(2,1)S(1)} collective-permute-done((bf16[128,1024]{1,0:T(8,128)(2,1)S(1)}, bf16[128,1024]{1,0:T(8,128)(2,1)S(1)}, u32[]{:S(2)}, u32[]{:S(2)}) %collective-permute-start.8) | collective-permute-done | bytes 262176 | tf_op jit(solution)/shard_map/ppermute | solution.py:121
  25.5 1.1 %collective-permute-done.6.refs_6_ = bf16[128,1024]{1,0:T(8,128)(2,1)S(1)} collective-permute-done((bf16[128,1024]{1,0:T(8,128)(2,1)S(1)}, bf16[128,1024]{1,0:T(8,128)(2,1)S(1)}, u32[]{:S(2)}, u32[]{:S(2)}) %collective-permute-start.6) | collective-permute-done | bytes 262176 | tf_op jit(solution)/shard_map/ppermute | solution.py:121
  26.6 5.2 %group_softmax.1 = (f32[128]{0:T(128)}, bf16[128,1024]{1,0:T(8,128)(2,1)}, bf16[128,1024]{1,0:T(8,128)(2,1)}) custom-call(bf16[128,1024]{1,0:T(8,128)(2,1)} %refs_0_.1, bf16[128,1024]{1,0:T(8,128)(2,1)S(1)} %collective-permute-done.refs_1_, bf16[128,1024]{1,0:T(8,128)(2,1)S(1)} %collective-permute-done.1.refs_2_, ...), custom_call_target="tpu_custom_call" | custom-call | tf_op jit(solution)/shard_map/group_softmax/pallas_call | solution.py:148
Async XLA Ops:
  0.6 6.2 %collective-permute-start.2 = (bf16[128,1024]{1,0:T(8,128)(2,1)}, bf16[128,1024]{1,0:T(8,128)(2,1)S(1)}, u32[]{:S(2)}, u32[]{:S(2)}) collective-permute-start(bf16[128,1024]{1,0:T(8,128)(2,1)} %refs_9_.1), channel_id=1, source_target_pairs={{0,1},{1,0},{2,3},{3,2},{4,5},{5,4},{6,7},{7,6},{8,9},{9,8},{10,11... | collective-permute-start | bytes 786440 | tf_op jit(solution)/shard_map/ppermute | solution.py:121
  1.1 9.9 %collective-permute-start = (bf16[128,1024]{1,0:T(8,128)(2,1)}, bf16[128,1024]{1,0:T(8,128)(2,1)S(1)}, u32[]{:S(2)}, u32[]{:S(2)}) collective-permute-start(bf16[128,1024]{1,0:T(8,128)(2,1)} %refs_0_.1), channel_id=1, source_target_pairs={{0,16},{1,9},{2,18},{3,11},{4,20},{5,13},{6,22},{7,15},{8,24},{9,1... | collective-permute-start | bytes 786440 | tf_op jit(solution)/shard_map/ppermute | solution.py:121
  4.8 9.5 %collective-permute-start.9 = (bf16[128,1024]{1,0:T(8,128)(2,1)}, bf16[128,1024]{1,0:T(8,128)(2,1)S(1)}, u32[]{:S(2)}, u32[]{:S(2)}) collective-permute-start(bf16[128,1024]{1,0:T(8,128)(2,1)} %refs_9_.1), channel_id=1, source_target_pairs={{0,2},{1,3},{2,0},{3,1},{4,6},{5,7},{6,4},{7,5},{8,10},{9,11},{10,... | collective-permute-start | bytes 786440 | tf_op jit(solution)/shard_map/ppermute | solution.py:121
  6.3 12.3 %collective-permute-start.12 = (bf16[128,1024]{1,0:T(8,128)(2,1)}, bf16[128,1024]{1,0:T(8,128)(2,1)S(1)}, u32[]{:S(2)}, u32[]{:S(2)}) collective-permute-start(bf16[128,1024]{1,0:T(8,128)(2,1)} %refs_13_.1), channel_id=1, source_target_pairs={{0,2},{1,3},{2,0},{3,1},{4,6},{5,7},{6,4},{7,5},{8,10},{9,11},{10,... | collective-permute-start | bytes 786440 | tf_op jit(solution)/shard_map/ppermute | solution.py:121
  6.8 13.4 %collective-permute-start.3 = (bf16[128,1024]{1,0:T(8,128)(2,1)}, bf16[128,1024]{1,0:T(8,128)(2,1)S(1)}, u32[]{:S(2)}, u32[]{:S(2)}) collective-permute-start(bf16[128,1024]{1,0:T(8,128)(2,1)} %refs_0_.1), channel_id=1, source_target_pairs={{0,28},{1,5},{2,30},{3,7},{4,24},{5,1},{6,26},{7,3},{8,20},{9,13},... | collective-permute-start | bytes 786440 | tf_op jit(solution)/shard_map/ppermute | solution.py:121
  14.3 5.9 %collective-permute-start.10 = (bf16[128,1024]{1,0:T(8,128)(2,1)S(1)}, bf16[128,1024]{1,0:T(8,128)(2,1)S(1)}, u32[]{:S(2)}, u32[]{:S(2)}) collective-permute-start(bf16[128,1024]{1,0:T(8,128)(2,1)S(1)} %collective-permute-done.9.refs_11_), channel_id=1, source_target_pairs={{0,1},{1,0},{2,3},{3,2},{4,5},{5,4},{6,7},{7,6},{8,9},{9,8},{10,11... | collective-permute-start | bytes 786440 | tf_op jit(solution)/shard_map/ppermute | solution.py:121
  14.3 6.5 %collective-permute-start.11 = (bf16[128,1024]{1,0:T(8,128)(2,1)}, bf16[128,1024]{1,0:T(8,128)(2,1)S(1)}, u32[]{:S(2)}, u32[]{:S(2)}) collective-permute-start(bf16[128,1024]{1,0:T(8,128)(2,1)} %refs_13_.1), channel_id=1, source_target_pairs={{0,1},{1,0},{2,3},{3,2},{4,5},{5,4},{6,7},{7,6},{8,9},{9,8},{10,11... | collective-permute-start | bytes 786440 | tf_op jit(solution)/shard_map/ppermute | solution.py:121
  14.8 8.3 %collective-permute-start.7 = (bf16[128,1024]{1,0:T(8,128)(2,1)S(1)}, bf16[128,1024]{1,0:T(8,128)(2,1)S(1)}, u32[]{:S(2)}, u32[]{:S(2)}) collective-permute-start(bf16[128,1024]{1,0:T(8,128)(2,1)S(1)} %collective-permute-done.refs_1_), channel_id=1, source_target_pairs={{0,8},{2,10},{4,12},{6,14},{8,0},{10,2},{12,4},{14,6},{16,24},{18,... | collective-permute-start | bytes 786440 | tf_op jit(solution)/shard_map/ppermute | solution.py:121
  18.6 6.4 %collective-permute-start.5 = (bf16[128,1024]{1,0:T(8,128)(2,1)S(1)}, bf16[128,1024]{1,0:T(8,128)(2,1)S(1)}, u32[]{:S(2)}, u32[]{:S(2)}) collective-permute-start(bf16[128,1024]{1,0:T(8,128)(2,1)S(1)} %collective-permute-done.refs_1_), channel_id=1, source_target_pairs={{0,4},{1,5},{2,6},{3,7},{4,0},{5,1},{6,2},{7,3},{8,12},{9,13},{10,... | collective-permute-start | bytes 786440 | tf_op jit(solution)/shard_map/ppermute | solution.py:121
  20.2 4.9 %collective-permute-start.13 = (bf16[128,1024]{1,0:T(8,128)(2,1)S(1)}, bf16[128,1024]{1,0:T(8,128)(2,1)S(1)}, u32[]{:S(2)}, u32[]{:S(2)}) collective-permute-start(bf16[128,1024]{1,0:T(8,128)(2,1)S(1)} %collective-permute-done.12.refs_15_), channel_id=1, source_target_pairs={{0,1},{1,0},{2,3},{3,2},{4,5},{5,4},{6,7},{7,6},{8,9},{9,8},{10,11... | collective-permute-start | bytes 786440 | tf_op jit(solution)/shard_map/ppermute | solution.py:121
  20.2 4.8 %collective-permute-start.1 = (bf16[128,1024]{1,0:T(8,128)(2,1)S(1)}, bf16[128,1024]{1,0:T(8,128)(2,1)S(1)}, u32[]{:S(2)}, u32[]{:S(2)}) collective-permute-start(bf16[128,1024]{1,0:T(8,128)(2,1)S(1)} %collective-permute-done.refs_1_), channel_id=1, source_target_pairs={{0,1},{1,0},{2,3},{3,2},{4,5},{5,4},{6,7},{7,6},{8,9},{9,8},{10,11... | collective-permute-start | bytes 786440 | tf_op jit(solution)/shard_map/ppermute | solution.py:121
  20.7 4.3 %collective-permute-start.4 = (bf16[128,1024]{1,0:T(8,128)(2,1)S(1)}, bf16[128,1024]{1,0:T(8,128)(2,1)S(1)}, u32[]{:S(2)}, u32[]{:S(2)}) collective-permute-start(bf16[128,1024]{1,0:T(8,128)(2,1)S(1)} %collective-permute-done.3.refs_3_), channel_id=1, source_target_pairs={{0,1},{1,0},{2,3},{3,2},{4,5},{5,4},{6,7},{7,6},{8,9},{9,8},{10,11... | collective-permute-start | bytes 786440 | tf_op jit(solution)/shard_map/ppermute | solution.py:121
  23.0 2.4 %collective-permute-start.8 = (bf16[128,1024]{1,0:T(8,128)(2,1)S(1)}, bf16[128,1024]{1,0:T(8,128)(2,1)S(1)}, u32[]{:S(2)}, u32[]{:S(2)}) collective-permute-start(bf16[128,1024]{1,0:T(8,128)(2,1)S(1)} %collective-permute-done.7.refs_7_), channel_id=1, source_target_pairs={{0,1},{2,3},{4,5},{6,7},{8,9},{10,11},{12,13},{14,15},{16,17},{18,... | collective-permute-start | bytes 786440 | tf_op jit(solution)/shard_map/ppermute | solution.py:121
  25.1 1.5 %collective-permute-start.6 = (bf16[128,1024]{1,0:T(8,128)(2,1)S(1)}, bf16[128,1024]{1,0:T(8,128)(2,1)S(1)}, u32[]{:S(2)}, u32[]{:S(2)}) collective-permute-start(bf16[128,1024]{1,0:T(8,128)(2,1)S(1)} %collective-permute-done.5.refs_5_), channel_id=1, source_target_pairs={{0,1},{1,0},{2,3},{3,2},{4,5},{5,4},{6,7},{7,6},{8,9},{9,8},{10,11... | collective-permute-start | bytes 786440 | tf_op jit(solution)/shard_map/ppermute | solution.py:121

commit v3 on v2

v3 whole, which is shorter than its diff:
```python
import functools
import math

import jax
import jax.numpy as jnp
from jax import lax
from jax.experimental import pallas as pl
from jax.experimental.pallas import tpu as pltpu
from jax.sharding import PartitionSpec as P

BLOCK = 512
LAST, FIRST = ((1,), (1,)), ((0,), (0,))


def dot(left, right, contract=((1,), (0,))):
    return lax.dot_general(left, right, (contract, ((), ())), preferred_element_type=jnp.float32)


def plan(dp):
    if dp == 8:
        return [(-1, (4, 2), (4, 2)), (-1, (0, 1), (0, 1)), (0, (1, 5), (5, 7)), (0, (2, 1), (6, 3))]
    return [(-1, (m, m + 1), (m, m + 1)) for m in range(0, dp, 2)]


def kernel(dp, rep, scale, slots, *refs):
    head_ref, refs = refs[0], refs[1:]
    pieces, refs = refs[: 2 * len(slots)], refs[2 * len(slots) :]
    entity_refs, refs = refs[:rep], refs[rep:]
    mention_refs, refs = refs[:rep], refs[rep:]
    loss_ref, mention_grad_ref, state_grad_ref = refs[:3]
    head, entities, mentions, projected, sems = refs[3:]

    rows, depth = entity_refs[0].shape[0], head_ref.shape[0]
    me, core = lax.axis_index("dp"), lax.rem(lax.axis_index("rep"), 2)

    copies = []

    def place(mask):
        at = pl.multiple_of(jnp.bitwise_xor(me, mask) * depth, depth)
        return head.at[pl.ds(at, depth)]

    def fetch(source, target):
        copies.append(pltpu.make_async_copy(source, target, sems.at[len(copies)]))
        copies[-1].start()

    for i in range(rep):
        fetch(entity_refs[i], entities.at[pl.ds(i * rows, rows)])
    fetch(head_ref, place(0))
    for i, (_, _, masks) in enumerate(slots):
        near, other = pieces[2 * i : 2 * i + 2]
        if masks[0] == 0:
            copies.append(pltpu.make_async_copy(near, place(masks[1]), sems.at[len(copies)]))
            pl.when(core == 1)(copies[-1].start)
            swapped = pltpu.make_async_copy(other, place(masks[1]), sems.at[len(copies) - 1])
            pl.when(core == 0)(swapped.start)
        else:
            fetch(near, place(jnp.where(core == 0, *masks)))
            fetch(other, place(jnp.where(core == 0, *masks[::-1])))
    ready = len(copies)
    for i in range(rep):
        fetch(mention_refs[i], mentions.at[pl.ds(i * rows, rows)])

    for copy in copies[:ready]:
        copy.wait()
    group, width = projected.shape
    step = min(width, 256)
    for at in range(0, width, step):
        projected[:, at : at + step] = dot(entities[...], head[:, at : at + step]).astype(jnp.bfloat16)
    for copy in copies[ready:]:
        copy.wait()

    block = min(group, BLOCK)
    summed = jnp.zeros((rows, width), jnp.float32)
    for at in range(0, group, block):
        part = mentions[at : at + block, :]
        scores = dot(part, projected[...], LAST) * scale
        top = jnp.max(scores, axis=1, keepdims=True)
        powers = jnp.exp(scores - top)
        total = jnp.sum(powers, axis=1, keepdims=True)
        chances = (powers / total).astype(jnp.bfloat16)
        summed += dot(chances[:, :rows], part, FIRST)
        if at == 0:
            log_total = top[:rows] + jnp.log(total[:rows])
            eye = lax.broadcasted_iota(jnp.int32, (rows, rows), 0) == lax.broadcasted_iota(
                jnp.int32, (rows, rows), 1
            )
            loss_ref[...] = jnp.sum(jnp.where(eye, log_total - scores[:rows, :rows], 0.0), axis=0)
            weighted = dot(chances[:rows], projected[...])
            mention_grad_ref[...] = (
                scale * (weighted - projected[:rows, :].astype(jnp.float32))
            ).astype(jnp.bfloat16)
    proj_grad = (scale * (summed - mentions[:rows, :].astype(jnp.float32))).astype(jnp.bfloat16)
    state_grad_ref[...] = dot(proj_grad, head[...], LAST).astype(jnp.bfloat16)


def solution(mesh):
    dp, rep = mesh.shape["dp"], mesh.shape["rep"]
    slots = plan(dp)

    def send(x, over_dp=(0, 0), over_rep=0):
        pairs = [
            (d * rep + r, (d ^ over_dp[r % 2]) * rep + (r ^ over_rep)) for d in range(dp) for r in range(rep)
        ]
        return lax.ppermute(x, ("dp", "rep"), pairs)

    def local(mentions, entity_states, head):
        rows, width = mentions.shape
        group = rep * rows
        entities, held = {0: entity_states}, {0: mentions}
        for store in (entities, held):
            store[1] = send(store[0], over_rep=1)
            for mask in range(2, rep, 2):
                store[mask] = send(store[0], over_rep=mask)
                store[mask + 1] = send(store[mask], over_rep=1)
        pieces = []
        for source, steps, _ in slots:
            near = send(head if source < 0 else pieces[2 * source], steps)
            pieces += [near, send(near, over_rep=1)]

        head, entities[0], held[0] = (
            pltpu.with_memory_space_constraint(x, pltpu.HBM) for x in (head, entities[0], held[0])
        )
        operands = [head] + pieces + [entities[i] for i in range(rep)] + [held[i] for i in range(rep)]
        anywhere = pl.BlockSpec(memory_space=pl.ANY)
        vmem = pl.BlockSpec(memory_space=pltpu.VMEM)
        return pl.pallas_call(
            functools.partial(kernel, dp, rep, 3.0 / math.sqrt(width), slots),
            out_shape=(
                jax.ShapeDtypeStruct((rows,), jnp.float32),
                jax.ShapeDtypeStruct((rows, width), jnp.bfloat16),
                jax.ShapeDtypeStruct((rows, width), jnp.bfloat16),
            ),
            in_specs=[anywhere] * len(operands),
            out_specs=(vmem, vmem, vmem),
            scratch_shapes=[
                pltpu.VMEM((dp * head.shape[0], width), jnp.bfloat16),
                pltpu.VMEM((group, width), jnp.bfloat16),
                pltpu.VMEM((group, width), jnp.bfloat16),
                pltpu.VMEM((group, width), jnp.bfloat16),
                pltpu.SemaphoreType.DMA((len(operands),)),
            ],
            compiler_params=pltpu.CompilerParams(vmem_limit_bytes=40 * 1024 * 1024),
            name="group_softmax",
        )(*operands)

    return jax.shard_map(
        local,
        mesh=mesh,
        in_specs=(P(("dp", "rep"), None), P(("dp", "rep"), None), P("dp", None)),
        out_specs=(P(("dp", "rep")), P(("dp", "rep"), None), P(("dp", "rep"), None)),
        check_vma=False,
    )
```

time: 32 us -> 30 us (0.938)
  starting transfers between devices: 16.3 us -> 11.9 us
  waiting for transfers between devices: 9.61 us -> 12.1 us
    ppermute x14, starting transfers between devices: 16.3 us -> 11.9 us  [send(): return lax.ppermute(x, ('dp', 'rep'), pairs)]
    ppermute x14, waiting for transfers between devices: 9.61 us -> 12.1 us  [send(): return lax.ppermute(x, ('dp', 'rep'), pairs)]
where the time goes in v3:
time: 30 us; the launch traced here: 29.8 us
  waiting for transfers between devices  12.1 us (40%)
  starting transfers between devices  11.9 us (40%)
  Pallas kernels  5.23 us (17%)
  between operations  0.64 us (2%)
    ppermute x14, waiting for transfers between devices, send(): return lax.ppermute(x, ('dp', 'rep'), pairs)  12.1 us
    ppermute x14, starting transfers between devices, send(): return lax.ppermute(x, ('dp', 'rep'), pairs)  11.9 us
    pallas_call x1, Pallas kernels, local(): pl.pallas_call(functools.partial(kernel, dp, rep, 3.0 / math.sqrt(width),...  5.23 us
  transfers between devices with their start and end apart: 14, of which 6 were waited for; matrix products, arithmetic and copies ran while one was open for 0% of the time, Pallas kernels for 0%

profile of v3, /device:TPU:0, one launch (start us, length us, event | category | flops | bytes accessed | tf_op | source)
XLA Modules:
  0.0 29.8 jit_solution(13579831350816605750)
XLA Ops:
  0.6 0.5 %collective-permute-start.11 = (bf16[128,1024]{1,0:T(8,128)(2,1)}, bf16[128,1024]{1,0:T(8,128)(2,1)S(1)}, u32[]{:S(2)}, u32[]{:S(2)}) collective-permute-start(bf16[128,1024]{1,0:T(8,128)(2,1)} %refs_13_.1), channel_id=1, source_target_pairs={{0,1},{1,0},{2,3},{3,2},{4,5},{5,4},{6,7},{7,6},{8,9},{9,8},{10,11... | collective-permute-start | bytes 786440 | tf_op jit(solution)/shard_map/ppermute | solution.py:104
  1.1 2.6 %collective-permute-start.12 = (bf16[128,1024]{1,0:T(8,128)(2,1)}, bf16[128,1024]{1,0:T(8,128)(2,1)S(1)}, u32[]{:S(2)}, u32[]{:S(2)}) collective-permute-start(bf16[128,1024]{1,0:T(8,128)(2,1)} %refs_13_.1), channel_id=1, source_target_pairs={{0,2},{1,3},{2,0},{3,1},{4,6},{5,7},{6,4},{7,5},{8,10},{9,11},{10,... | collective-permute-start | bytes 786440 | tf_op jit(solution)/shard_map/ppermute | solution.py:104
  3.7 2.6 %collective-permute-start = (bf16[128,1024]{1,0:T(8,128)(2,1)}, bf16[128,1024]{1,0:T(8,128)(2,1)S(1)}, u32[]{:S(2)}, u32[]{:S(2)}) collective-permute-start(bf16[128,1024]{1,0:T(8,128)(2,1)} %refs_0_.1), channel_id=1, source_target_pairs={{0,16},{1,9},{2,18},{3,11},{4,20},{5,13},{6,22},{7,15},{8,24},{9,1... | collective-permute-start | bytes 786440 | tf_op jit(solution)/shard_map/ppermute | solution.py:104
  6.3 0.0 collective-permute-start.8
  6.3 0.5 %collective-permute-start.9 = (bf16[128,1024]{1,0:T(8,128)(2,1)}, bf16[128,1024]{1,0:T(8,128)(2,1)S(1)}, u32[]{:S(2)}, u32[]{:S(2)}) collective-permute-start(bf16[128,1024]{1,0:T(8,128)(2,1)} %refs_9_.1), channel_id=1, source_target_pairs={{0,2},{1,3},{2,0},{3,1},{4,6},{5,7},{6,4},{7,5},{8,10},{9,11},{10,... | collective-permute-start | bytes 786440 | tf_op jit(solution)/shard_map/ppermute | solution.py:104
  6.8 0.0 collective-permute-done.11.refs_14_
  6.8 1.6 %collective-permute-start.2 = (bf16[128,1024]{1,0:T(8,128)(2,1)}, bf16[128,1024]{1,0:T(8,128)(2,1)S(1)}, u32[]{:S(2)}, u32[]{:S(2)}) collective-permute-start(bf16[128,1024]{1,0:T(8,128)(2,1)} %refs_0_.1), channel_id=1, source_target_pairs={{0,0},{1,5},{2,2},{3,7},{4,4},{5,1},{6,6},{7,3},{8,8},{9,13},{10,1... | collective-permute-start | bytes 786440 | tf_op jit(solution)/shard_map/ppermute | solution.py:104
  8.4 2.6 %collective-permute-done.12.refs_15_ = bf16[128,1024]{1,0:T(8,128)(2,1)S(1)} collective-permute-done((bf16[128,1024]{1,0:T(8,128)(2,1)}, bf16[128,1024]{1,0:T(8,128)(2,1)S(1)}, u32[]{:S(2)}, u32[]{:S(2)}) %collective-permute-start.12) | collective-permute-done | bytes 262176 | tf_op jit(solution)/shard_map/ppermute | solution.py:104
  11.1 0.0 collective-permute-start.13
  11.1 2.0 %collective-permute-done.refs_1_ = bf16[128,1024]{1,0:T(8,128)(2,1)S(1)} collective-permute-done((bf16[128,1024]{1,0:T(8,128)(2,1)}, bf16[128,1024]{1,0:T(8,128)(2,1)S(1)}, u32[]{:S(2)}, u32[]{:S(2)}) %collective-permute-start) | collective-permute-done | bytes 262176 | tf_op jit(solution)/shard_map/ppermute | solution.py:104
  13.1 1.8 %collective-permute-start.6 = (bf16[128,1024]{1,0:T(8,128)(2,1)S(1)}, bf16[128,1024]{1,0:T(8,128)(2,1)S(1)}, u32[]{:S(2)}, u32[]{:S(2)}) collective-permute-start(bf16[128,1024]{1,0:T(8,128)(2,1)S(1)} %collective-permute-done.refs_1_), channel_id=1, source_target_pairs={{0,8},{1,5},{2,10},{3,7},{4,12},{5,1},{6,14},{7,3},{8,0},{9,13},{1... | collective-permute-start | bytes 786440 | tf_op jit(solution)/shard_map/ppermute | solution.py:104
  14.9 0.0 collective-permute-done.8.refs_10_
  14.9 1.5 %collective-permute-start.4 = (bf16[128,1024]{1,0:T(8,128)(2,1)S(1)}, bf16[128,1024]{1,0:T(8,128)(2,1)S(1)}, u32[]{:S(2)}, u32[]{:S(2)}) collective-permute-start(bf16[128,1024]{1,0:T(8,128)(2,1)S(1)} %collective-permute-done.refs_1_), channel_id=1, source_target_pairs={{0,4},{1,21},{2,6},{3,23},{4,0},{5,17},{6,2},{7,19},{8,12},{9,29},... | collective-permute-start | bytes 786440 | tf_op jit(solution)/shard_map/ppermute | solution.py:104
  16.4 0.0 collective-permute-done.9.refs_11_
  16.4 0.0 collective-permute-start.1
  16.4 0.0 collective-permute-done.2.refs_3_
  16.4 0.5 %collective-permute-start.10 = (bf16[128,1024]{1,0:T(8,128)(2,1)S(1)}, bf16[128,1024]{1,0:T(8,128)(2,1)S(1)}, u32[]{:S(2)}, u32[]{:S(2)}) collective-permute-start(bf16[128,1024]{1,0:T(8,128)(2,1)S(1)} %collective-permute-done.9.refs_11_), channel_id=1, source_target_pairs={{0,1},{1,0},{2,3},{3,2},{4,5},{5,4},{6,7},{7,6},{8,9},{9,8},{10,11... | collective-permute-start | bytes 786440 | tf_op jit(solution)/shard_map/ppermute | solution.py:104
  17.0 0.0 collective-permute-done.13.refs_16_
  17.0 0.1 collective-permute-start.3
  17.0 4.8 %collective-permute-done.6.refs_7_ = bf16[128,1024]{1,0:T(8,128)(2,1)S(1)} collective-permute-done((bf16[128,1024]{1,0:T(8,128)(2,1)S(1)}, bf16[128,1024]{1,0:T(8,128)(2,1)S(1)}, u32[]{:S(2)}, u32[]{:S(2)}) %collective-permute-start.6) | collective-permute-done | bytes 262176 | tf_op jit(solution)/shard_map/ppermute | solution.py:104
  21.8 0.0 collective-permute-start.7
  21.8 1.2 %collective-permute-done.4.refs_5_ = bf16[128,1024]{1,0:T(8,128)(2,1)S(1)} collective-permute-done((bf16[128,1024]{1,0:T(8,128)(2,1)S(1)}, bf16[128,1024]{1,0:T(8,128)(2,1)S(1)}, u32[]{:S(2)}, u32[]{:S(2)}) %collective-permute-start.4) | collective-permute-done | bytes 262176 | tf_op jit(solution)/shard_map/ppermute | solution.py:104
  23.0 0.2 collective-permute-start.5
  23.2 0.0 collective-permute-done.10.refs_12_
  23.2 0.0 collective-permute-done.1.refs_2_
  23.2 0.0 collective-permute-done.3.refs_4_
  23.2 0.1 collective-permute-done.7.refs_8_
  23.4 1.2 %collective-permute-done.5.refs_6_ = bf16[128,1024]{1,0:T(8,128)(2,1)S(1)} collective-permute-done((bf16[128,1024]{1,0:T(8,128)(2,1)S(1)}, bf16[128,1024]{1,0:T(8,128)(2,1)S(1)}, u32[]{:S(2)}, u32[]{:S(2)}) %collective-permute-start.5) | collective-permute-done | bytes 262176 | tf_op jit(solution)/shard_map/ppermute | solution.py:104
  24.6 5.2 %group_softmax.1 = (f32[128]{0:T(128)}, bf16[128,1024]{1,0:T(8,128)(2,1)}, bf16[128,1024]{1,0:T(8,128)(2,1)}) custom-call(bf16[128,1024]{1,0:T(8,128)(2,1)} %refs_0_.1, bf16[128,1024]{1,0:T(8,128)(2,1)S(1)} %collective-permute-done.refs_1_, bf16[128,1024]{1,0:T(8,128)(2,1)S(1)} %collective-permute-done.1.refs_2_, ...), custom_call_target="tpu_custom_call" | custom-call | tf_op jit(solution)/shard_map/group_softmax/pallas_call | solution.py:126
Async XLA Ops:
  0.6 6.2 %collective-permute-start.11 = (bf16[128,1024]{1,0:T(8,128)(2,1)}, bf16[128,1024]{1,0:T(8,128)(2,1)S(1)}, u32[]{:S(2)}, u32[]{:S(2)}) collective-permute-start(bf16[128,1024]{1,0:T(8,128)(2,1)} %refs_13_.1), channel_id=1, source_target_pairs={{0,1},{1,0},{2,3},{3,2},{4,5},{5,4},{6,7},{7,6},{8,9},{9,8},{10,11... | collective-permute-start | bytes 786440 | tf_op jit(solution)/shard_map/ppermute | solution.py:104
  1.1 9.9 %collective-permute-start.12 = (bf16[128,1024]{1,0:T(8,128)(2,1)}, bf16[128,1024]{1,0:T(8,128)(2,1)S(1)}, u32[]{:S(2)}, u32[]{:S(2)}) collective-permute-start(bf16[128,1024]{1,0:T(8,128)(2,1)} %refs_13_.1), channel_id=1, source_target_pairs={{0,2},{1,3},{2,0},{3,1},{4,6},{5,7},{6,4},{7,5},{8,10},{9,11},{10,... | collective-permute-start | bytes 786440 | tf_op jit(solution)/shard_map/ppermute | solution.py:104
  3.7 9.4 %collective-permute-start = (bf16[128,1024]{1,0:T(8,128)(2,1)}, bf16[128,1024]{1,0:T(8,128)(2,1)S(1)}, u32[]{:S(2)}, u32[]{:S(2)}) collective-permute-start(bf16[128,1024]{1,0:T(8,128)(2,1)} %refs_0_.1), channel_id=1, source_target_pairs={{0,16},{1,9},{2,18},{3,11},{4,20},{5,13},{6,22},{7,15},{8,24},{9,1... | collective-permute-start | bytes 786440 | tf_op jit(solution)/shard_map/ppermute | solution.py:104
  6.3 8.6 %collective-permute-start.8 = (bf16[128,1024]{1,0:T(8,128)(2,1)}, bf16[128,1024]{1,0:T(8,128)(2,1)S(1)}, u32[]{:S(2)}, u32[]{:S(2)}) collective-permute-start(bf16[128,1024]{1,0:T(8,128)(2,1)} %refs_9_.1), channel_id=1, source_target_pairs={{0,1},{1,0},{2,3},{3,2},{4,5},{5,4},{6,7},{7,6},{8,9},{9,8},{10,11... | collective-permute-start | bytes 786440 | tf_op jit(solution)/shard_map/ppermute | solution.py:104
  6.3 10.1 %collective-permute-start.9 = (bf16[128,1024]{1,0:T(8,128)(2,1)}, bf16[128,1024]{1,0:T(8,128)(2,1)S(1)}, u32[]{:S(2)}, u32[]{:S(2)}) collective-permute-start(bf16[128,1024]{1,0:T(8,128)(2,1)} %refs_9_.1), channel_id=1, source_target_pairs={{0,2},{1,3},{2,0},{3,1},{4,6},{5,7},{6,4},{7,5},{8,10},{9,11},{10,... | collective-permute-start | bytes 786440 | tf_op jit(solution)/shard_map/ppermute | solution.py:104
  6.8 9.6 %collective-permute-start.2 = (bf16[128,1024]{1,0:T(8,128)(2,1)}, bf16[128,1024]{1,0:T(8,128)(2,1)S(1)}, u32[]{:S(2)}, u32[]{:S(2)}) collective-permute-start(bf16[128,1024]{1,0:T(8,128)(2,1)} %refs_0_.1), channel_id=1, source_target_pairs={{0,0},{1,5},{2,2},{3,7},{4,4},{5,1},{6,6},{7,3},{8,8},{9,13},{10,1... | collective-permute-start | bytes 786440 | tf_op jit(solution)/shard_map/ppermute | solution.py:104
  11.1 5.9 %collective-permute-start.13 = (bf16[128,1024]{1,0:T(8,128)(2,1)S(1)}, bf16[128,1024]{1,0:T(8,128)(2,1)S(1)}, u32[]{:S(2)}, u32[]{:S(2)}) collective-permute-start(bf16[128,1024]{1,0:T(8,128)(2,1)S(1)} %collective-permute-done.12.refs_15_), channel_id=1, source_target_pairs={{0,1},{1,0},{2,3},{3,2},{4,5},{5,4},{6,7},{7,6},{8,9},{9,8},{10,11... | collective-permute-start | bytes 786440 | tf_op jit(solution)/shard_map/ppermute | solution.py:104
  13.1 8.7 %collective-permute-start.6 = (bf16[128,1024]{1,0:T(8,128)(2,1)S(1)}, bf16[128,1024]{1,0:T(8,128)(2,1)S(1)}, u32[]{:S(2)}, u32[]{:S(2)}) collective-permute-start(bf16[128,1024]{1,0:T(8,128)(2,1)S(1)} %collective-permute-done.refs_1_), channel_id=1, source_target_pairs={{0,8},{1,5},{2,10},{3,7},{4,12},{5,1},{6,14},{7,3},{8,0},{9,13},{1... | collective-permute-start | bytes 786440 | tf_op jit(solution)/shard_map/ppermute | solution.py:104
  14.9 8.2 %collective-permute-start.4 = (bf16[128,1024]{1,0:T(8,128)(2,1)S(1)}, bf16[128,1024]{1,0:T(8,128)(2,1)S(1)}, u32[]{:S(2)}, u32[]{:S(2)}) collective-permute-start(bf16[128,1024]{1,0:T(8,128)(2,1)S(1)} %collective-permute-done.refs_1_), channel_id=1, source_target_pairs={{0,4},{1,21},{2,6},{3,23},{4,0},{5,17},{6,2},{7,19},{8,12},{9,29},... | collective-permute-start | bytes 786440 | tf_op jit(solution)/shard_map/ppermute | solution.py:104
  16.4 6.8 %collective-permute-start.1 = (bf16[128,1024]{1,0:T(8,128)(2,1)S(1)}, bf16[128,1024]{1,0:T(8,128)(2,1)S(1)}, u32[]{:S(2)}, u32[]{:S(2)}) collective-permute-start(bf16[128,1024]{1,0:T(8,128)(2,1)S(1)} %collective-permute-done.refs_1_), channel_id=1, source_target_pairs={{0,1},{1,0},{2,3},{3,2},{4,5},{5,4},{6,7},{7,6},{8,9},{9,8},{10,11... | collective-permute-start | bytes 786440 | tf_op jit(solution)/shard_map/ppermute | solution.py:104
  16.4 6.8 %collective-permute-start.10 = (bf16[128,1024]{1,0:T(8,128)(2,1)S(1)}, bf16[128,1024]{1,0:T(8,128)(2,1)S(1)}, u32[]{:S(2)}, u32[]{:S(2)}) collective-permute-start(bf16[128,1024]{1,0:T(8,128)(2,1)S(1)} %collective-permute-done.9.refs_11_), channel_id=1, source_target_pairs={{0,1},{1,0},{2,3},{3,2},{4,5},{5,4},{6,7},{7,6},{8,9},{9,8},{10,11... | collective-permute-start | bytes 786440 | tf_op jit(solution)/shard_map/ppermute | solution.py:104
  17.0 6.3 %collective-permute-start.3 = (bf16[128,1024]{1,0:T(8,128)(2,1)S(1)}, bf16[128,1024]{1,0:T(8,128)(2,1)S(1)}, u32[]{:S(2)}, u32[]{:S(2)}) collective-permute-start(bf16[128,1024]{1,0:T(8,128)(2,1)S(1)} %collective-permute-done.2.refs_3_), channel_id=1, source_target_pairs={{0,1},{1,0},{2,3},{3,2},{4,5},{5,4},{6,7},{7,6},{8,9},{9,8},{10,11... | collective-permute-start | bytes 786440 | tf_op jit(solution)/shard_map/ppermute | solution.py:104
  21.8 1.5 %collective-permute-start.7 = (bf16[128,1024]{1,0:T(8,128)(2,1)S(1)}, bf16[128,1024]{1,0:T(8,128)(2,1)S(1)}, u32[]{:S(2)}, u32[]{:S(2)}) collective-permute-start(bf16[128,1024]{1,0:T(8,128)(2,1)S(1)} %collective-permute-done.6.refs_7_), channel_id=1, source_target_pairs={{0,1},{1,0},{2,3},{3,2},{4,5},{5,4},{6,7},{7,6},{8,9},{9,8},{10,11... | collective-permute-start | bytes 786440 | tf_op jit(solution)/shard_map/ppermute | solution.py:104
  23.0 1.5 %collective-permute-start.5 = (bf16[128,1024]{1,0:T(8,128)(2,1)S(1)}, bf16[128,1024]{1,0:T(8,128)(2,1)S(1)}, u32[]{:S(2)}, u32[]{:S(2)}) collective-permute-start(bf16[128,1024]{1,0:T(8,128)(2,1)S(1)} %collective-permute-done.4.refs_5_), channel_id=1, source_target_pairs={{0,1},{1,0},{2,3},{3,2},{4,5},{5,4},{6,7},{7,6},{8,9},{9,8},{10,11... | collective-permute-start | bytes 786440 | tf_op jit(solution)/shard_map/ppermute | solution.py:104

commit v4 on v3

--- a/solution.py
+++ b/solution.py
@@ -23,14 +23,13 @@
 
 
 def kernel(dp, rep, scale, slots, *refs):
-    head_ref, refs = refs[0], refs[1:]
-    pieces, refs = refs[: 2 * len(slots)], refs[2 * len(slots) :]
+    pieces, refs = refs[1 : 2 * len(slots) + 1], refs[2 * len(slots) + 1 :]
     entity_refs, refs = refs[:rep], refs[rep:]
     mention_refs, refs = refs[:rep], refs[rep:]
     loss_ref, mention_grad_ref, state_grad_ref = refs[:3]
     head, entities, mentions, projected, sems = refs[3:]
 
-    rows, depth = entity_refs[0].shape[0], head_ref.shape[0]
+    rows, depth = entity_refs[0].shape[0], pieces[0].shape[0]
     me, core = lax.axis_index("dp"), lax.rem(lax.axis_index("rep"), 2)
 
     copies = []
@@ -43,29 +42,27 @@
         copies.append(pltpu.make_async_copy(source, target, sems.at[len(copies)]))
         copies[-1].start()
 
-    for i in range(rep):
+    fetch(entity_refs[0], entities.at[pl.ds(0, rows)])
+    fetch(mention_refs[0], mentions.at[pl.ds(0, rows)])
+    for i in range(1, rep):
         fetch(entity_refs[i], entities.at[pl.ds(i * rows, rows)])
-    fetch(head_ref, place(0))
     for i, (_, _, masks) in enumerate(slots):
-        near, other = pieces[2 * i : 2 * i + 2]
-        if masks[0] == 0:
-            copies.append(pltpu.make_async_copy(near, place(masks[1]), sems.at[len(copies)]))
-            pl.when(core == 1)(copies[-1].start)
-            swapped = pltpu.make_async_copy(other, place(masks[1]), sems.at[len(copies) - 1])
-            pl.when(core == 0)(swapped.start)
-        else:
-            fetch(near, place(jnp.where(core == 0, *masks)))
-            fetch(other, place(jnp.where(core == 0, *masks[::-1])))
+        fetch(pieces[2 * i], place(jnp.where(core == 0, *masks)))
+        fetch(pieces[2 * i + 1], place(jnp.where(core == 0, *masks[::-1])))
     ready = len(copies)
-    for i in range(rep):
+    for i in range(1, rep):
         fetch(mention_refs[i], mentions.at[pl.ds(i * rows, rows)])
 
-    for copy in copies[:ready]:
+    for copy in copies[2:ready]:
         copy.wait()
     group, width = projected.shape
     step = min(width, 256)
-    for at in range(0, width, step):
-        projected[:, at : at + step] = dot(entities[...], head[:, at : at + step]).astype(jnp.bfloat16)
+    for to in (slice(rows, group), slice(0, rows)):
+        if to.start == 0:
+            copies[0].wait()
+        for at in range(0, width, step):
+            projected[to, at : at + step] = dot(entities[to, :], head[:, at : at + step]).astype(jnp.bfloat16)
+    copies[1].wait()
     for copy in copies[ready:]:
         copy.wait()
 

time: 30 us -> 29.4 us (0.980)
  Pallas kernels: 5.23 us -> 4.67 us
    pallas_call x1, Pallas kernels: 5.23 us -> 4.67 us  [local(): pl.pallas_call(functools.partial(kernel, dp, rep, 3.0 / math.sqrt(width),...]
where the time goes in v4:
time: 29.4 us; the launch traced here: 29.3 us
  waiting for transfers between devices  12.1 us (41%)
  starting transfers between devices  11.9 us (40%)
  Pallas kernels  4.67 us (16%)
  between operations  0.64 us (2%)
    ppermute x14, waiting for transfers between devices, send(): return lax.ppermute(x, ('dp', 'rep'), pairs)  12.1 us
    ppermute x14, starting transfers between devices, send(): return lax.ppermute(x, ('dp', 'rep'), pairs)  11.9 us
    pallas_call x1, Pallas kernels, local(): pl.pallas_call(functools.partial(kernel, dp, rep, 3.0 / math.sqrt(width),...  4.67 us
  transfers between devices with their start and end apart: 14, of which 6 were waited for; matrix products, arithmetic and copies ran while one was open for 0% of the time, Pallas kernels for 0%

profile of v4, /device:TPU:0, one launch (start us, length us, event | category | flops | bytes accessed | tf_op | source)
XLA Modules:
  0.0 29.3 jit_solution(15106828505240693779)
XLA Ops:
  0.6 0.5 %collective-permute-start.11 = (bf16[128,1024]{1,0:T(8,128)(2,1)}, bf16[128,1024]{1,0:T(8,128)(2,1)S(1)}, u32[]{:S(2)}, u32[]{:S(2)}) collective-permute-start(bf16[128,1024]{1,0:T(8,128)(2,1)} %refs_13_.1), channel_id=1, source_target_pairs={{0,1},{1,0},{2,3},{3,2},{4,5},{5,4},{6,7},{7,6},{8,9},{9,8},{10,11... | collective-permute-start | bytes 786440 | tf_op jit(solution)/shard_map/ppermute | solution.py:101
  1.1 2.6 %collective-permute-start.12 = (bf16[128,1024]{1,0:T(8,128)(2,1)}, bf16[128,1024]{1,0:T(8,128)(2,1)S(1)}, u32[]{:S(2)}, u32[]{:S(2)}) collective-permute-start(bf16[128,1024]{1,0:T(8,128)(2,1)} %refs_13_.1), channel_id=1, source_target_pairs={{0,2},{1,3},{2,0},{3,1},{4,6},{5,7},{6,4},{7,5},{8,10},{9,11},{10,... | collective-permute-start | bytes 786440 | tf_op jit(solution)/shard_map/ppermute | solution.py:101
  3.7 2.6 %collective-permute-start = (bf16[128,1024]{1,0:T(8,128)(2,1)}, bf16[128,1024]{1,0:T(8,128)(2,1)S(1)}, u32[]{:S(2)}, u32[]{:S(2)}) collective-permute-start(bf16[128,1024]{1,0:T(8,128)(2,1)} %refs_0_.1), channel_id=1, source_target_pairs={{0,16},{1,9},{2,18},{3,11},{4,20},{5,13},{6,22},{7,15},{8,24},{9,1... | collective-permute-start | bytes 786440 | tf_op jit(solution)/shard_map/ppermute | solution.py:101
  6.3 0.0 collective-permute-start.8
  6.3 0.5 %collective-permute-start.9 = (bf16[128,1024]{1,0:T(8,128)(2,1)}, bf16[128,1024]{1,0:T(8,128)(2,1)S(1)}, u32[]{:S(2)}, u32[]{:S(2)}) collective-permute-start(bf16[128,1024]{1,0:T(8,128)(2,1)} %refs_9_.1), channel_id=1, source_target_pairs={{0,2},{1,3},{2,0},{3,1},{4,6},{5,7},{6,4},{7,5},{8,10},{9,11},{10,... | collective-permute-start | bytes 786440 | tf_op jit(solution)/shard_map/ppermute | solution.py:101
  6.8 0.0 collective-permute-done.11.refs_14_
  6.8 1.6 %collective-permute-start.2 = (bf16[128,1024]{1,0:T(8,128)(2,1)}, bf16[128,1024]{1,0:T(8,128)(2,1)S(1)}, u32[]{:S(2)}, u32[]{:S(2)}) collective-permute-start(bf16[128,1024]{1,0:T(8,128)(2,1)} %refs_0_.1), channel_id=1, source_target_pairs={{0,0},{1,5},{2,2},{3,7},{4,4},{5,1},{6,6},{7,3},{8,8},{9,13},{10,1... | collective-permute-start | bytes 786440 | tf_op jit(solution)/shard_map/ppermute | solution.py:101
  8.4 2.6 %collective-permute-done.12.refs_15_ = bf16[128,1024]{1,0:T(8,128)(2,1)S(1)} collective-permute-done((bf16[128,1024]{1,0:T(8,128)(2,1)}, bf16[128,1024]{1,0:T(8,128)(2,1)S(1)}, u32[]{:S(2)}, u32[]{:S(2)}) %collective-permute-start.12) | collective-permute-done | bytes 262176 | tf_op jit(solution)/shard_map/ppermute | solution.py:101
  11.1 0.0 collective-permute-start.13
  11.1 2.0 %collective-permute-done.refs_1_ = bf16[128,1024]{1,0:T(8,128)(2,1)S(1)} collective-permute-done((bf16[128,1024]{1,0:T(8,128)(2,1)}, bf16[128,1024]{1,0:T(8,128)(2,1)S(1)}, u32[]{:S(2)}, u32[]{:S(2)}) %collective-permute-start) | collective-permute-done | bytes 262176 | tf_op jit(solution)/shard_map/ppermute | solution.py:101
  13.1 1.8 %collective-permute-start.6 = (bf16[128,1024]{1,0:T(8,128)(2,1)S(1)}, bf16[128,1024]{1,0:T(8,128)(2,1)S(1)}, u32[]{:S(2)}, u32[]{:S(2)}) collective-permute-start(bf16[128,1024]{1,0:T(8,128)(2,1)S(1)} %collective-permute-done.refs_1_), channel_id=1, source_target_pairs={{0,8},{1,5},{2,10},{3,7},{4,12},{5,1},{6,14},{7,3},{8,0},{9,13},{1... | collective-permute-start | bytes 786440 | tf_op jit(solution)/shard_map/ppermute | solution.py:101
  14.9 0.0 collective-permute-done.8.refs_10_
  14.9 1.5 %collective-permute-start.4 = (bf16[128,1024]{1,0:T(8,128)(2,1)S(1)}, bf16[128,1024]{1,0:T(8,128)(2,1)S(1)}, u32[]{:S(2)}, u32[]{:S(2)}) collective-permute-start(bf16[128,1024]{1,0:T(8,128)(2,1)S(1)} %collective-permute-done.refs_1_), channel_id=1, source_target_pairs={{0,4},{1,21},{2,6},{3,23},{4,0},{5,17},{6,2},{7,19},{8,12},{9,29},... | collective-permute-start | bytes 786440 | tf_op jit(solution)/shard_map/ppermute | solution.py:101
  16.4 0.0 collective-permute-done.9.refs_11_
  16.4 0.0 collective-permute-start.1
  16.4 0.0 collective-permute-done.2.refs_3_
  16.4 0.5 %collective-permute-start.10 = (bf16[128,1024]{1,0:T(8,128)(2,1)S(1)}, bf16[128,1024]{1,0:T(8,128)(2,1)S(1)}, u32[]{:S(2)}, u32[]{:S(2)}) collective-permute-start(bf16[128,1024]{1,0:T(8,128)(2,1)S(1)} %collective-permute-done.9.refs_11_), channel_id=1, source_target_pairs={{0,1},{1,0},{2,3},{3,2},{4,5},{5,4},{6,7},{7,6},{8,9},{9,8},{10,11... | collective-permute-start | bytes 786440 | tf_op jit(solution)/shard_map/ppermute | solution.py:101
  17.0 0.0 collective-permute-done.13.refs_16_
  17.0 0.1 collective-permute-start.3
  17.0 4.8 %collective-permute-done.6.refs_7_ = bf16[128,1024]{1,0:T(8,128)(2,1)S(1)} collective-permute-done((bf16[128,1024]{1,0:T(8,128)(2,1)S(1)}, bf16[128,1024]{1,0:T(8,128)(2,1)S(1)}, u32[]{:S(2)}, u32[]{:S(2)}) %collective-permute-start.6) | collective-permute-done | bytes 262176 | tf_op jit(solution)/shard_map/ppermute | solution.py:101
  21.8 0.0 collective-permute-start.7
  21.8 1.2 %collective-permute-done.4.refs_5_ = bf16[128,1024]{1,0:T(8,128)(2,1)S(1)} collective-permute-done((bf16[128,1024]{1,0:T(8,128)(2,1)S(1)}, bf16[128,1024]{1,0:T(8,128)(2,1)S(1)}, u32[]{:S(2)}, u32[]{:S(2)}) %collective-permute-start.4) | collective-permute-done | bytes 262176 | tf_op jit(solution)/shard_map/ppermute | solution.py:101
  23.0 0.2 collective-permute-start.5
  23.2 0.0 collective-permute-done.10.refs_12_
  23.2 0.0 collective-permute-done.1.refs_2_
  23.2 0.0 collective-permute-done.3.refs_4_
  23.2 0.1 collective-permute-done.7.refs_8_
  23.4 1.2 %collective-permute-done.5.refs_6_ = bf16[128,1024]{1,0:T(8,128)(2,1)S(1)} collective-permute-done((bf16[128,1024]{1,0:T(8,128)(2,1)S(1)}, bf16[128,1024]{1,0:T(8,128)(2,1)S(1)}, u32[]{:S(2)}, u32[]{:S(2)}) %collective-permute-start.5) | collective-permute-done | bytes 262176 | tf_op jit(solution)/shard_map/ppermute | solution.py:101
  24.6 4.7 %group_softmax.1 = (f32[128]{0:T(128)}, bf16[128,1024]{1,0:T(8,128)(2,1)}, bf16[128,1024]{1,0:T(8,128)(2,1)}) custom-call(bf16[128,1024]{1,0:T(8,128)(2,1)} %refs_0_.1, bf16[128,1024]{1,0:T(8,128)(2,1)S(1)} %collective-permute-done.refs_1_, bf16[128,1024]{1,0:T(8,128)(2,1)S(1)} %collective-permute-done.1.refs_2_, ...), custom_call_target="tpu_custom_call" | custom-call | tf_op jit(solution)/shard_map/group_softmax/pallas_call | solution.py:123
Async XLA Ops:
  0.6 6.2 %collective-permute-start.11 = (bf16[128,1024]{1,0:T(8,128)(2,1)}, bf16[128,1024]{1,0:T(8,128)(2,1)S(1)}, u32[]{:S(2)}, u32[]{:S(2)}) collective-permute-start(bf16[128,1024]{1,0:T(8,128)(2,1)} %refs_13_.1), channel_id=1, source_target_pairs={{0,1},{1,0},{2,3},{3,2},{4,5},{5,4},{6,7},{7,6},{8,9},{9,8},{10,11... | collective-permute-start | bytes 786440 | tf_op jit(solution)/shard_map/ppermute | solution.py:101
  1.1 9.9 %collective-permute-start.12 = (bf16[128,1024]{1,0:T(8,128)(2,1)}, bf16[128,1024]{1,0:T(8,128)(2,1)S(1)}, u32[]{:S(2)}, u32[]{:S(2)}) collective-permute-start(bf16[128,1024]{1,0:T(8,128)(2,1)} %refs_13_.1), channel_id=1, source_target_pairs={{0,2},{1,3},{2,0},{3,1},{4,6},{5,7},{6,4},{7,5},{8,10},{9,11},{10,... | collective-permute-start | bytes 786440 | tf_op jit(solution)/shard_map/ppermute | solution.py:101
  3.7 9.4 %collective-permute-start = (bf16[128,1024]{1,0:T(8,128)(2,1)}, bf16[128,1024]{1,0:T(8,128)(2,1)S(1)}, u32[]{:S(2)}, u32[]{:S(2)}) collective-permute-start(bf16[128,1024]{1,0:T(8,128)(2,1)} %refs_0_.1), channel_id=1, source_target_pairs={{0,16},{1,9},{2,18},{3,11},{4,20},{5,13},{6,22},{7,15},{8,24},{9,1... | collective-permute-start | bytes 786440 | tf_op jit(solution)/shard_map/ppermute | solution.py:101
  6.3 8.6 %collective-permute-start.8 = (bf16[128,1024]{1,0:T(8,128)(2,1)}, bf16[128,1024]{1,0:T(8,128)(2,1)S(1)}, u32[]{:S(2)}, u32[]{:S(2)}) collective-permute-start(bf16[128,1024]{1,0:T(8,128)(2,1)} %refs_9_.1), channel_id=1, source_target_pairs={{0,1},{1,0},{2,3},{3,2},{4,5},{5,4},{6,7},{7,6},{8,9},{9,8},{10,11... | collective-permute-start | bytes 786440 | tf_op jit(solution)/shard_map/ppermute | solution.py:101
  6.3 10.1 %collective-permute-start.9 = (bf16[128,1024]{1,0:T(8,128)(2,1)}, bf16[128,1024]{1,0:T(8,128)(2,1)S(1)}, u32[]{:S(2)}, u32[]{:S(2)}) collective-permute-start(bf16[128,1024]{1,0:T(8,128)(2,1)} %refs_9_.1), channel_id=1, source_target_pairs={{0,2},{1,3},{2,0},{3,1},{4,6},{5,7},{6,4},{7,5},{8,10},{9,11},{10,... | collective-permute-start | bytes 786440 | tf_op jit(solution)/shard_map/ppermute | solution.py:101
  6.8 9.6 %collective-permute-start.2 = (bf16[128,1024]{1,0:T(8,128)(2,1)}, bf16[128,1024]{1,0:T(8,128)(2,1)S(1)}, u32[]{:S(2)}, u32[]{:S(2)}) collective-permute-start(bf16[128,1024]{1,0:T(8,128)(2,1)} %refs_0_.1), channel_id=1, source_target_pairs={{0,0},{1,5},{2,2},{3,7},{4,4},{5,1},{6,6},{7,3},{8,8},{9,13},{10,1... | collective-permute-start | bytes 786440 | tf_op jit(solution)/shard_map/ppermute | solution.py:101
  11.1 5.9 %collective-permute-start.13 = (bf16[128,1024]{1,0:T(8,128)(2,1)S(1)}, bf16[128,1024]{1,0:T(8,128)(2,1)S(1)}, u32[]{:S(2)}, u32[]{:S(2)}) collective-permute-start(bf16[128,1024]{1,0:T(8,128)(2,1)S(1)} %collective-permute-done.12.refs_15_), channel_id=1, source_target_pairs={{0,1},{1,0},{2,3},{3,2},{4,5},{5,4},{6,7},{7,6},{8,9},{9,8},{10,11... | collective-permute-start | bytes 786440 | tf_op jit(solution)/shard_map/ppermute | solution.py:101
  13.1 8.7 %collective-permute-start.6 = (bf16[128,1024]{1,0:T(8,128)(2,1)S(1)}, bf16[128,1024]{1,0:T(8,128)(2,1)S(1)}, u32[]{:S(2)}, u32[]{:S(2)}) collective-permute-start(bf16[128,1024]{1,0:T(8,128)(2,1)S(1)} %collective-permute-done.refs_1_), channel_id=1, source_target_pairs={{0,8},{1,5},{2,10},{3,7},{4,12},{5,1},{6,14},{7,3},{8,0},{9,13},{1... | collective-permute-start | bytes 786440 | tf_op jit(solution)/shard_map/ppermute | solution.py:101
  14.9 8.2 %collective-permute-start.4 = (bf16[128,1024]{1,0:T(8,128)(2,1)S(1)}, bf16[128,1024]{1,0:T(8,128)(2,1)S(1)}, u32[]{:S(2)}, u32[]{:S(2)}) collective-permute-start(bf16[128,1024]{1,0:T(8,128)(2,1)S(1)} %collective-permute-done.refs_1_), channel_id=1, source_target_pairs={{0,4},{1,21},{2,6},{3,23},{4,0},{5,17},{6,2},{7,19},{8,12},{9,29},... | collective-permute-start | bytes 786440 | tf_op jit(solution)/shard_map/ppermute | solution.py:101
  16.4 6.8 %collective-permute-start.1 = (bf16[128,1024]{1,0:T(8,128)(2,1)S(1)}, bf16[128,1024]{1,0:T(8,128)(2,1)S(1)}, u32[]{:S(2)}, u32[]{:S(2)}) collective-permute-start(bf16[128,1024]{1,0:T(8,128)(2,1)S(1)} %collective-permute-done.refs_1_), channel_id=1, source_target_pairs={{0,1},{1,0},{2,3},{3,2},{4,5},{5,4},{6,7},{7,6},{8,9},{9,8},{10,11... | collective-permute-start | bytes 786440 | tf_op jit(solution)/shard_map/ppermute | solution.py:101
  16.4 6.8 %collective-permute-start.10 = (bf16[128,1024]{1,0:T(8,128)(2,1)S(1)}, bf16[128,1024]{1,0:T(8,128)(2,1)S(1)}, u32[]{:S(2)}, u32[]{:S(2)}) collective-permute-start(bf16[128,1024]{1,0:T(8,128)(2,1)S(1)} %collective-permute-done.9.refs_11_), channel_id=1, source_target_pairs={{0,1},{1,0},{2,3},{3,2},{4,5},{5,4},{6,7},{7,6},{8,9},{9,8},{10,11... | collective-permute-start | bytes 786440 | tf_op jit(solution)/shard_map/ppermute | solution.py:101
  17.0 6.3 %collective-permute-start.3 = (bf16[128,1024]{1,0:T(8,128)(2,1)S(1)}, bf16[128,1024]{1,0:T(8,128)(2,1)S(1)}, u32[]{:S(2)}, u32[]{:S(2)}) collective-permute-start(bf16[128,1024]{1,0:T(8,128)(2,1)S(1)} %collective-permute-done.2.refs_3_), channel_id=1, source_target_pairs={{0,1},{1,0},{2,3},{3,2},{4,5},{5,4},{6,7},{7,6},{8,9},{9,8},{10,11... | collective-permute-start | bytes 786440 | tf_op jit(solution)/shard_map/ppermute | solution.py:101
  21.8 1.5 %collective-permute-start.7 = (bf16[128,1024]{1,0:T(8,128)(2,1)S(1)}, bf16[128,1024]{1,0:T(8,128)(2,1)S(1)}, u32[]{:S(2)}, u32[]{:S(2)}) collective-permute-start(bf16[128,1024]{1,0:T(8,128)(2,1)S(1)} %collective-permute-done.6.refs_7_), channel_id=1, source_target_pairs={{0,1},{1,0},{2,3},{3,2},{4,5},{5,4},{6,7},{7,6},{8,9},{9,8},{10,11... | collective-permute-start | bytes 786440 | tf_op jit(solution)/shard_map/ppermute | solution.py:101
  23.0 1.5 %collective-permute-start.5 = (bf16[128,1024]{1,0:T(8,128)(2,1)S(1)}, bf16[128,1024]{1,0:T(8,128)(2,1)S(1)}, u32[]{:S(2)}, u32[]{:S(2)}) collective-permute-start(bf16[128,1024]{1,0:T(8,128)(2,1)S(1)} %collective-permute-done.4.refs_5_), channel_id=1, source_target_pairs={{0,1},{1,0},{2,3},{3,2},{4,5},{5,4},{6,7},{7,6},{8,9},{9,8},{10,11... | collective-permute-start | bytes 786440 | tf_op jit(solution)/shard_map/ppermute | solution.py:101

commit v5 on v4

--- a/solution.py
+++ b/solution.py
@@ -44,8 +44,6 @@
 
     fetch(entity_refs[0], entities.at[pl.ds(0, rows)])
     fetch(mention_refs[0], mentions.at[pl.ds(0, rows)])
-    for i in range(1, rep):
-        fetch(entity_refs[i], entities.at[pl.ds(i * rows, rows)])
     for i, (_, _, masks) in enumerate(slots):
         fetch(pieces[2 * i], place(jnp.where(core == 0, *masks)))
         fetch(pieces[2 * i + 1], place(jnp.where(core == 0, *masks[::-1])))
@@ -56,12 +54,13 @@
     for copy in copies[2:ready]:
         copy.wait()
     group, width = projected.shape
-    step = min(width, 256)
+    step = min(width, 512)
     for to in (slice(rows, group), slice(0, rows)):
         if to.start == 0:
             copies[0].wait()
         for at in range(0, width, step):
-            projected[to, at : at + step] = dot(entities[to, :], head[:, at : at + step]).astype(jnp.bfloat16)
+            part = entities[...] if to.start == 0 else jnp.concatenate([ref[...] for ref in entity_refs[1:]], axis=0)
+            projected[to, at : at + step] = dot(part, head[:, at : at + step]).astype(jnp.bfloat16)
     copies[1].wait()
     for copy in copies[ready:]:
         copy.wait()
@@ -127,11 +126,11 @@
                 jax.ShapeDtypeStruct((rows, width), jnp.bfloat16),
                 jax.ShapeDtypeStruct((rows, width), jnp.bfloat16),
             ),
-            in_specs=[anywhere] * len(operands),
+            in_specs=[anywhere] * (len(pieces) + 2) + [vmem] * (rep - 1) + [anywhere] * rep,
             out_specs=(vmem, vmem, vmem),
             scratch_shapes=[
                 pltpu.VMEM((dp * head.shape[0], width), jnp.bfloat16),
-                pltpu.VMEM((group, width), jnp.bfloat16),
+                pltpu.VMEM((rows, width), jnp.bfloat16),
                 pltpu.VMEM((group, width), jnp.bfloat16),
                 pltpu.VMEM((group, width), jnp.bfloat16),
                 pltpu.SemaphoreType.DMA((len(operands),)),

time: 29.4 us -> 29.4 us (level)
  no operation moved by 1% of the time
where the time goes in v5:
time: 29.4 us; the launch traced here: 29.2 us
  waiting for transfers between devices  12.1 us (41%)
  starting transfers between devices  11.9 us (40%)
  Pallas kernels  4.61 us (16%)
  between operations  0.64 us (2%)
    ppermute x14, waiting for transfers between devices, send(): return lax.ppermute(x, ('dp', 'rep'), pairs)  12.1 us
    ppermute x14, starting transfers between devices, send(): return lax.ppermute(x, ('dp', 'rep'), pairs)  11.9 us
    pallas_call x1, Pallas kernels, local(): pl.pallas_call(functools.partial(kernel, dp, rep, 3.0 / math.sqrt(width),...  4.61 us
  transfers between devices with their start and end apart: 14, of which 6 were waited for; matrix products, arithmetic and copies ran while one was open for 0% of the time, Pallas kernels for 0%

profile of v5, /device:TPU:0, one launch (start us, length us, event | category | flops | bytes accessed | tf_op | source)
XLA Modules:
  0.0 29.2 jit_solution(16092317015559871715)
XLA Ops:
  0.6 0.5 %collective-permute-start.11 = (bf16[128,1024]{1,0:T(8,128)(2,1)}, bf16[128,1024]{1,0:T(8,128)(2,1)S(1)}, u32[]{:S(2)}, u32[]{:S(2)}) collective-permute-start(bf16[128,1024]{1,0:T(8,128)(2,1)} %refs_13_.1), channel_id=1, source_target_pairs={{0,1},{1,0},{2,3},{3,2},{4,5},{5,4},{6,7},{7,6},{8,9},{9,8},{10,11... | collective-permute-start | bytes 786440 | tf_op jit(solution)/shard_map/ppermute | solution.py:100
  1.1 2.6 %collective-permute-start.12 = (bf16[128,1024]{1,0:T(8,128)(2,1)}, bf16[128,1024]{1,0:T(8,128)(2,1)S(1)}, u32[]{:S(2)}, u32[]{:S(2)}) collective-permute-start(bf16[128,1024]{1,0:T(8,128)(2,1)} %refs_13_.1), channel_id=1, source_target_pairs={{0,2},{1,3},{2,0},{3,1},{4,6},{5,7},{6,4},{7,5},{8,10},{9,11},{10,... | collective-permute-start | bytes 786440 | tf_op jit(solution)/shard_map/ppermute | solution.py:100
  3.7 2.6 %collective-permute-start = (bf16[128,1024]{1,0:T(8,128)(2,1)}, bf16[128,1024]{1,0:T(8,128)(2,1)S(1)}, u32[]{:S(2)}, u32[]{:S(2)}) collective-permute-start(bf16[128,1024]{1,0:T(8,128)(2,1)} %refs_0_.1), channel_id=1, source_target_pairs={{0,16},{1,9},{2,18},{3,11},{4,20},{5,13},{6,22},{7,15},{8,24},{9,1... | collective-permute-start | bytes 786440 | tf_op jit(solution)/shard_map/ppermute | solution.py:100
  6.3 0.0 collective-permute-start.8
  6.3 0.5 %collective-permute-start.9 = (bf16[128,1024]{1,0:T(8,128)(2,1)}, bf16[128,1024]{1,0:T(8,128)(2,1)S(1)}, u32[]{:S(2)}, u32[]{:S(2)}) collective-permute-start(bf16[128,1024]{1,0:T(8,128)(2,1)} %refs_9_.1), channel_id=1, source_target_pairs={{0,2},{1,3},{2,0},{3,1},{4,6},{5,7},{6,4},{7,5},{8,10},{9,11},{10,... | collective-permute-start | bytes 786440 | tf_op jit(solution)/shard_map/ppermute | solution.py:100
  6.8 0.0 collective-permute-done.11.refs_14_
  6.8 1.6 %collective-permute-start.2 = (bf16[128,1024]{1,0:T(8,128)(2,1)}, bf16[128,1024]{1,0:T(8,128)(2,1)S(1)}, u32[]{:S(2)}, u32[]{:S(2)}) collective-permute-start(bf16[128,1024]{1,0:T(8,128)(2,1)} %refs_0_.1), channel_id=1, source_target_pairs={{0,0},{1,5},{2,2},{3,7},{4,4},{5,1},{6,6},{7,3},{8,8},{9,13},{10,1... | collective-permute-start | bytes 786440 | tf_op jit(solution)/shard_map/ppermute | solution.py:100
  8.4 2.6 %collective-permute-done.12.refs_15_ = bf16[128,1024]{1,0:T(8,128)(2,1)S(1)} collective-permute-done((bf16[128,1024]{1,0:T(8,128)(2,1)}, bf16[128,1024]{1,0:T(8,128)(2,1)S(1)}, u32[]{:S(2)}, u32[]{:S(2)}) %collective-permute-start.12) | collective-permute-done | bytes 262176 | tf_op jit(solution)/shard_map/ppermute | solution.py:100
  11.1 0.0 collective-permute-start.13
  11.1 2.0 %collective-permute-done.refs_1_ = bf16[128,1024]{1,0:T(8,128)(2,1)S(1)} collective-permute-done((bf16[128,1024]{1,0:T(8,128)(2,1)}, bf16[128,1024]{1,0:T(8,128)(2,1)S(1)}, u32[]{:S(2)}, u32[]{:S(2)}) %collective-permute-start) | collective-permute-done | bytes 262176 | tf_op jit(solution)/shard_map/ppermute | solution.py:100
  13.1 1.8 %collective-permute-start.6 = (bf16[128,1024]{1,0:T(8,128)(2,1)S(1)}, bf16[128,1024]{1,0:T(8,128)(2,1)S(1)}, u32[]{:S(2)}, u32[]{:S(2)}) collective-permute-start(bf16[128,1024]{1,0:T(8,128)(2,1)S(1)} %collective-permute-done.refs_1_), channel_id=1, source_target_pairs={{0,8},{1,5},{2,10},{3,7},{4,12},{5,1},{6,14},{7,3},{8,0},{9,13},{1... | collective-permute-start | bytes 786440 | tf_op jit(solution)/shard_map/ppermute | solution.py:100
  14.9 0.0 collective-permute-done.8.refs_10_
  14.9 1.5 %collective-permute-start.4 = (bf16[128,1024]{1,0:T(8,128)(2,1)S(1)}, bf16[128,1024]{1,0:T(8,128)(2,1)S(1)}, u32[]{:S(2)}, u32[]{:S(2)}) collective-permute-start(bf16[128,1024]{1,0:T(8,128)(2,1)S(1)} %collective-permute-done.refs_1_), channel_id=1, source_target_pairs={{0,4},{1,21},{2,6},{3,23},{4,0},{5,17},{6,2},{7,19},{8,12},{9,29},... | collective-permute-start | bytes 786440 | tf_op jit(solution)/shard_map/ppermute | solution.py:100
  16.4 0.0 collective-permute-done.9.refs_11_
  16.4 0.0 collective-permute-start.1
  16.4 0.0 collective-permute-done.2.refs_3_
  16.4 0.5 %collective-permute-start.10 = (bf16[128,1024]{1,0:T(8,128)(2,1)S(1)}, bf16[128,1024]{1,0:T(8,128)(2,1)S(1)}, u32[]{:S(2)}, u32[]{:S(2)}) collective-permute-start(bf16[128,1024]{1,0:T(8,128)(2,1)S(1)} %collective-permute-done.9.refs_11_), channel_id=1, source_target_pairs={{0,1},{1,0},{2,3},{3,2},{4,5},{5,4},{6,7},{7,6},{8,9},{9,8},{10,11... | collective-permute-start | bytes 786440 | tf_op jit(solution)/shard_map/ppermute | solution.py:100
  17.0 0.0 collective-permute-done.13.refs_16_
  17.0 0.1 collective-permute-start.3
  17.0 4.8 %collective-permute-done.6.refs_7_ = bf16[128,1024]{1,0:T(8,128)(2,1)S(1)} collective-permute-done((bf16[128,1024]{1,0:T(8,128)(2,1)S(1)}, bf16[128,1024]{1,0:T(8,128)(2,1)S(1)}, u32[]{:S(2)}, u32[]{:S(2)}) %collective-permute-start.6) | collective-permute-done | bytes 262176 | tf_op jit(solution)/shard_map/ppermute | solution.py:100
  21.8 0.0 collective-permute-start.7
  21.8 1.2 %collective-permute-done.4.refs_5_ = bf16[128,1024]{1,0:T(8,128)(2,1)S(1)} collective-permute-done((bf16[128,1024]{1,0:T(8,128)(2,1)S(1)}, bf16[128,1024]{1,0:T(8,128)(2,1)S(1)}, u32[]{:S(2)}, u32[]{:S(2)}) %collective-permute-start.4) | collective-permute-done | bytes 262176 | tf_op jit(solution)/shard_map/ppermute | solution.py:100
  23.0 0.2 collective-permute-start.5
  23.2 0.0 collective-permute-done.10.refs_12_
  23.2 0.0 collective-permute-done.1.refs_2_
  23.2 0.0 collective-permute-done.3.refs_4_
  23.2 0.1 collective-permute-done.7.refs_8_
  23.4 1.2 %collective-permute-done.5.refs_6_ = bf16[128,1024]{1,0:T(8,128)(2,1)S(1)} collective-permute-done((bf16[128,1024]{1,0:T(8,128)(2,1)S(1)}, bf16[128,1024]{1,0:T(8,128)(2,1)S(1)}, u32[]{:S(2)}, u32[]{:S(2)}) %collective-permute-start.5) | collective-permute-done | bytes 262176 | tf_op jit(solution)/shard_map/ppermute | solution.py:100
  24.6 4.6 %group_softmax.1 = (f32[128]{0:T(128)}, bf16[128,1024]{1,0:T(8,128)(2,1)}, bf16[128,1024]{1,0:T(8,128)(2,1)}) custom-call(bf16[128,1024]{1,0:T(8,128)(2,1)} %refs_0_.1, bf16[128,1024]{1,0:T(8,128)(2,1)S(1)} %collective-permute-done.refs_1_, bf16[128,1024]{1,0:T(8,128)(2,1)S(1)} %collective-permute-done.1.refs_2_, ...), custom_call_target="tpu_custom_call" | custom-call | tf_op jit(solution)/shard_map/group_softmax/pallas_call | solution.py:122
Async XLA Ops:
  0.6 6.2 %collective-permute-start.11 = (bf16[128,1024]{1,0:T(8,128)(2,1)}, bf16[128,1024]{1,0:T(8,128)(2,1)S(1)}, u32[]{:S(2)}, u32[]{:S(2)}) collective-permute-start(bf16[128,1024]{1,0:T(8,128)(2,1)} %refs_13_.1), channel_id=1, source_target_pairs={{0,1},{1,0},{2,3},{3,2},{4,5},{5,4},{6,7},{7,6},{8,9},{9,8},{10,11... | collective-permute-start | bytes 786440 | tf_op jit(solution)/shard_map/ppermute | solution.py:100
  1.1 9.9 %collective-permute-start.12 = (bf16[128,1024]{1,0:T(8,128)(2,1)}, bf16[128,1024]{1,0:T(8,128)(2,1)S(1)}, u32[]{:S(2)}, u32[]{:S(2)}) collective-permute-start(bf16[128,1024]{1,0:T(8,128)(2,1)} %refs_13_.1), channel_id=1, source_target_pairs={{0,2},{1,3},{2,0},{3,1},{4,6},{5,7},{6,4},{7,5},{8,10},{9,11},{10,... | collective-permute-start | bytes 786440 | tf_op jit(solution)/shard_map/ppermute | solution.py:100
  3.7 9.4 %collective-permute-start = (bf16[128,1024]{1,0:T(8,128)(2,1)}, bf16[128,1024]{1,0:T(8,128)(2,1)S(1)}, u32[]{:S(2)}, u32[]{:S(2)}) collective-permute-start(bf16[128,1024]{1,0:T(8,128)(2,1)} %refs_0_.1), channel_id=1, source_target_pairs={{0,16},{1,9},{2,18},{3,11},{4,20},{5,13},{6,22},{7,15},{8,24},{9,1... | collective-permute-start | bytes 786440 | tf_op jit(solution)/shard_map/ppermute | solution.py:100
  6.3 8.6 %collective-permute-start.8 = (bf16[128,1024]{1,0:T(8,128)(2,1)}, bf16[128,1024]{1,0:T(8,128)(2,1)S(1)}, u32[]{:S(2)}, u32[]{:S(2)}) collective-permute-start(bf16[128,1024]{1,0:T(8,128)(2,1)} %refs_9_.1), channel_id=1, source_target_pairs={{0,1},{1,0},{2,3},{3,2},{4,5},{5,4},{6,7},{7,6},{8,9},{9,8},{10,11... | collective-permute-start | bytes 786440 | tf_op jit(solution)/shard_map/ppermute | solution.py:100
  6.3 10.1 %collective-permute-start.9 = (bf16[128,1024]{1,0:T(8,128)(2,1)}, bf16[128,1024]{1,0:T(8,128)(2,1)S(1)}, u32[]{:S(2)}, u32[]{:S(2)}) collective-permute-start(bf16[128,1024]{1,0:T(8,128)(2,1)} %refs_9_.1), channel_id=1, source_target_pairs={{0,2},{1,3},{2,0},{3,1},{4,6},{5,7},{6,4},{7,5},{8,10},{9,11},{10,... | collective-permute-start | bytes 786440 | tf_op jit(solution)/shard_map/ppermute | solution.py:100
  6.8 9.6 %collective-permute-start.2 = (bf16[128,1024]{1,0:T(8,128)(2,1)}, bf16[128,1024]{1,0:T(8,128)(2,1)S(1)}, u32[]{:S(2)}, u32[]{:S(2)}) collective-permute-start(bf16[128,1024]{1,0:T(8,128)(2,1)} %refs_0_.1), channel_id=1, source_target_pairs={{0,0},{1,5},{2,2},{3,7},{4,4},{5,1},{6,6},{7,3},{8,8},{9,13},{10,1... | collective-permute-start | bytes 786440 | tf_op jit(solution)/shard_map/ppermute | solution.py:100
  11.1 5.9 %collective-permute-start.13 = (bf16[128,1024]{1,0:T(8,128)(2,1)S(1)}, bf16[128,1024]{1,0:T(8,128)(2,1)S(1)}, u32[]{:S(2)}, u32[]{:S(2)}) collective-permute-start(bf16[128,1024]{1,0:T(8,128)(2,1)S(1)} %collective-permute-done.12.refs_15_), channel_id=1, source_target_pairs={{0,1},{1,0},{2,3},{3,2},{4,5},{5,4},{6,7},{7,6},{8,9},{9,8},{10,11... | collective-permute-start | bytes 786440 | tf_op jit(solution)/shard_map/ppermute | solution.py:100
  13.1 8.7 %collective-permute-start.6 = (bf16[128,1024]{1,0:T(8,128)(2,1)S(1)}, bf16[128,1024]{1,0:T(8,128)(2,1)S(1)}, u32[]{:S(2)}, u32[]{:S(2)}) collective-permute-start(bf16[128,1024]{1,0:T(8,128)(2,1)S(1)} %collective-permute-done.refs_1_), channel_id=1, source_target_pairs={{0,8},{1,5},{2,10},{3,7},{4,12},{5,1},{6,14},{7,3},{8,0},{9,13},{1... | collective-permute-start | bytes 786440 | tf_op jit(solution)/shard_map/ppermute | solution.py:100
  14.9 8.2 %collective-permute-start.4 = (bf16[128,1024]{1,0:T(8,128)(2,1)S(1)}, bf16[128,1024]{1,0:T(8,128)(2,1)S(1)}, u32[]{:S(2)}, u32[]{:S(2)}) collective-permute-start(bf16[128,1024]{1,0:T(8,128)(2,1)S(1)} %collective-permute-done.refs_1_), channel_id=1, source_target_pairs={{0,4},{1,21},{2,6},{3,23},{4,0},{5,17},{6,2},{7,19},{8,12},{9,29},... | collective-permute-start | bytes 786440 | tf_op jit(solution)/shard_map/ppermute | solution.py:100
  16.4 6.8 %collective-permute-start.1 = (bf16[128,1024]{1,0:T(8,128)(2,1)S(1)}, bf16[128,1024]{1,0:T(8,128)(2,1)S(1)}, u32[]{:S(2)}, u32[]{:S(2)}) collective-permute-start(bf16[128,1024]{1,0:T(8,128)(2,1)S(1)} %collective-permute-done.refs_1_), channel_id=1, source_target_pairs={{0,1},{1,0},{2,3},{3,2},{4,5},{5,4},{6,7},{7,6},{8,9},{9,8},{10,11... | collective-permute-start | bytes 786440 | tf_op jit(solution)/shard_map/ppermute | solution.py:100
  16.4 6.8 %collective-permute-start.10 = (bf16[128,1024]{1,0:T(8,128)(2,1)S(1)}, bf16[128,1024]{1,0:T(8,128)(2,1)S(1)}, u32[]{:S(2)}, u32[]{:S(2)}) collective-permute-start(bf16[128,1024]{1,0:T(8,128)(2,1)S(1)} %collective-permute-done.9.refs_11_), channel_id=1, source_target_pairs={{0,1},{1,0},{2,3},{3,2},{4,5},{5,4},{6,7},{7,6},{8,9},{9,8},{10,11... | collective-permute-start | bytes 786440 | tf_op jit(solution)/shard_map/ppermute | solution.py:100
  17.0 6.3 %collective-permute-start.3 = (bf16[128,1024]{1,0:T(8,128)(2,1)S(1)}, bf16[128,1024]{1,0:T(8,128)(2,1)S(1)}, u32[]{:S(2)}, u32[]{:S(2)}) collective-permute-start(bf16[128,1024]{1,0:T(8,128)(2,1)S(1)} %collective-permute-done.2.refs_3_), channel_id=1, source_target_pairs={{0,1},{1,0},{2,3},{3,2},{4,5},{5,4},{6,7},{7,6},{8,9},{9,8},{10,11... | collective-permute-start | bytes 786440 | tf_op jit(solution)/shard_map/ppermute | solution.py:100
  21.8 1.5 %collective-permute-start.7 = (bf16[128,1024]{1,0:T(8,128)(2,1)S(1)}, bf16[128,1024]{1,0:T(8,128)(2,1)S(1)}, u32[]{:S(2)}, u32[]{:S(2)}) collective-permute-start(bf16[128,1024]{1,0:T(8,128)(2,1)S(1)} %collective-permute-done.6.refs_7_), channel_id=1, source_target_pairs={{0,1},{1,0},{2,3},{3,2},{4,5},{5,4},{6,7},{7,6},{8,9},{9,8},{10,11... | collective-permute-start | bytes 786440 | tf_op jit(solution)/shard_map/ppermute | solution.py:100
  23.0 1.5 %collective-permute-start.5 = (bf16[128,1024]{1,0:T(8,128)(2,1)S(1)}, bf16[128,1024]{1,0:T(8,128)(2,1)S(1)}, u32[]{:S(2)}, u32[]{:S(2)}) collective-permute-start(bf16[128,1024]{1,0:T(8,128)(2,1)S(1)} %collective-permute-done.4.refs_5_), channel_id=1, source_target_pairs={{0,1},{1,0},{2,3},{3,2},{4,5},{5,4},{6,7},{7,6},{8,9},{9,8},{10,11... | collective-permute-start | bytes 786440 | tf_op jit(solution)/shard_map/ppermute | solution.py:100

commit v6 on v4

--- a/solution.py
+++ b/solution.py
@@ -56,7 +56,7 @@
     for copy in copies[2:ready]:
         copy.wait()
     group, width = projected.shape
-    step = min(width, 256)
+    step = min(width, 512)
     for to in (slice(rows, group), slice(0, rows)):
         if to.start == 0:
             copies[0].wait()

time: 29.4 us -> 29.4 us (level)
  no operation moved by 1% of the time
where the time goes in v6:
time: 29.4 us; the launch traced here: 29.3 us
  waiting for transfers between devices  12.1 us (41%)
  starting transfers between devices  11.9 us (40%)
  Pallas kernels  4.67 us (16%)
  between operations  0.64 us (2%)
    ppermute x14, waiting for transfers between devices, send(): return lax.ppermute(x, ('dp', 'rep'), pairs)  12.1 us
    ppermute x14, starting transfers between devices, send(): return lax.ppermute(x, ('dp', 'rep'), pairs)  11.9 us
    pallas_call x1, Pallas kernels, local(): pl.pallas_call(functools.partial(kernel, dp, rep, 3.0 / math.sqrt(width),...  4.67 us
  transfers between devices with their start and end apart: 14, of which 6 were waited for; matrix products, arithmetic and copies ran while one was open for 0% of the time, Pallas kernels for 0%

profile of v6, /device:TPU:0, one launch (start us, length us, event | category | flops | bytes accessed | tf_op | source)
XLA Modules:
  0.0 29.3 jit_solution(15106828505240693779)
XLA Ops:
  0.6 0.5 %collective-permute-start.11 = (bf16[128,1024]{1,0:T(8,128)(2,1)}, bf16[128,1024]{1,0:T(8,128)(2,1)S(1)}, u32[]{:S(2)}, u32[]{:S(2)}) collective-permute-start(bf16[128,1024]{1,0:T(8,128)(2,1)} %refs_13_.1), channel_id=1, source_target_pairs={{0,1},{1,0},{2,3},{3,2},{4,5},{5,4},{6,7},{7,6},{8,9},{9,8},{10,11... | collective-permute-start | bytes 786440 | tf_op jit(solution)/shard_map/ppermute | solution.py:101
  1.1 2.6 %collective-permute-start.12 = (bf16[128,1024]{1,0:T(8,128)(2,1)}, bf16[128,1024]{1,0:T(8,128)(2,1)S(1)}, u32[]{:S(2)}, u32[]{:S(2)}) collective-permute-start(bf16[128,1024]{1,0:T(8,128)(2,1)} %refs_13_.1), channel_id=1, source_target_pairs={{0,2},{1,3},{2,0},{3,1},{4,6},{5,7},{6,4},{7,5},{8,10},{9,11},{10,... | collective-permute-start | bytes 786440 | tf_op jit(solution)/shard_map/ppermute | solution.py:101
  3.7 2.6 %collective-permute-start = (bf16[128,1024]{1,0:T(8,128)(2,1)}, bf16[128,1024]{1,0:T(8,128)(2,1)S(1)}, u32[]{:S(2)}, u32[]{:S(2)}) collective-permute-start(bf16[128,1024]{1,0:T(8,128)(2,1)} %refs_0_.1), channel_id=1, source_target_pairs={{0,16},{1,9},{2,18},{3,11},{4,20},{5,13},{6,22},{7,15},{8,24},{9,1... | collective-permute-start | bytes 786440 | tf_op jit(solution)/shard_map/ppermute | solution.py:101
  6.3 0.0 collective-permute-start.8
  6.3 0.5 %collective-permute-start.9 = (bf16[128,1024]{1,0:T(8,128)(2,1)}, bf16[128,1024]{1,0:T(8,128)(2,1)S(1)}, u32[]{:S(2)}, u32[]{:S(2)}) collective-permute-start(bf16[128,1024]{1,0:T(8,128)(2,1)} %refs_9_.1), channel_id=1, source_target_pairs={{0,2},{1,3},{2,0},{3,1},{4,6},{5,7},{6,4},{7,5},{8,10},{9,11},{10,... | collective-permute-start | bytes 786440 | tf_op jit(solution)/shard_map/ppermute | solution.py:101
  6.8 0.0 collective-permute-done.11.refs_14_
  6.8 1.6 %collective-permute-start.2 = (bf16[128,1024]{1,0:T(8,128)(2,1)}, bf16[128,1024]{1,0:T(8,128)(2,1)S(1)}, u32[]{:S(2)}, u32[]{:S(2)}) collective-permute-start(bf16[128,1024]{1,0:T(8,128)(2,1)} %refs_0_.1), channel_id=1, source_target_pairs={{0,0},{1,5},{2,2},{3,7},{4,4},{5,1},{6,6},{7,3},{8,8},{9,13},{10,1... | collective-permute-start | bytes 786440 | tf_op jit(solution)/shard_map/ppermute | solution.py:101
  8.4 2.6 %collective-permute-done.12.refs_15_ = bf16[128,1024]{1,0:T(8,128)(2,1)S(1)} collective-permute-done((bf16[128,1024]{1,0:T(8,128)(2,1)}, bf16[128,1024]{1,0:T(8,128)(2,1)S(1)}, u32[]{:S(2)}, u32[]{:S(2)}) %collective-permute-start.12) | collective-permute-done | bytes 262176 | tf_op jit(solution)/shard_map/ppermute | solution.py:101
  11.1 0.0 collective-permute-start.13
  11.1 2.0 %collective-permute-done.refs_1_ = bf16[128,1024]{1,0:T(8,128)(2,1)S(1)} collective-permute-done((bf16[128,1024]{1,0:T(8,128)(2,1)}, bf16[128,1024]{1,0:T(8,128)(2,1)S(1)}, u32[]{:S(2)}, u32[]{:S(2)}) %collective-permute-start) | collective-permute-done | bytes 262176 | tf_op jit(solution)/shard_map/ppermute | solution.py:101
  13.1 1.8 %collective-permute-start.6 = (bf16[128,1024]{1,0:T(8,128)(2,1)S(1)}, bf16[128,1024]{1,0:T(8,128)(2,1)S(1)}, u32[]{:S(2)}, u32[]{:S(2)}) collective-permute-start(bf16[128,1024]{1,0:T(8,128)(2,1)S(1)} %collective-permute-done.refs_1_), channel_id=1, source_target_pairs={{0,8},{1,5},{2,10},{3,7},{4,12},{5,1},{6,14},{7,3},{8,0},{9,13},{1... | collective-permute-start | bytes 786440 | tf_op jit(solution)/shard_map/ppermute | solution.py:101
  14.9 0.0 collective-permute-done.8.refs_10_
  14.9 1.5 %collective-permute-start.4 = (bf16[128,1024]{1,0:T(8,128)(2,1)S(1)}, bf16[128,1024]{1,0:T(8,128)(2,1)S(1)}, u32[]{:S(2)}, u32[]{:S(2)}) collective-permute-start(bf16[128,1024]{1,0:T(8,128)(2,1)S(1)} %collective-permute-done.refs_1_), channel_id=1, source_target_pairs={{0,4},{1,21},{2,6},{3,23},{4,0},{5,17},{6,2},{7,19},{8,12},{9,29},... | collective-permute-start | bytes 786440 | tf_op jit(solution)/shard_map/ppermute | solution.py:101
  16.4 0.0 collective-permute-done.9.refs_11_
  16.4 0.0 collective-permute-start.1
  16.4 0.0 collective-permute-done.2.refs_3_
  16.4 0.5 %collective-permute-start.10 = (bf16[128,1024]{1,0:T(8,128)(2,1)S(1)}, bf16[128,1024]{1,0:T(8,128)(2,1)S(1)}, u32[]{:S(2)}, u32[]{:S(2)}) collective-permute-start(bf16[128,1024]{1,0:T(8,128)(2,1)S(1)} %collective-permute-done.9.refs_11_), channel_id=1, source_target_pairs={{0,1},{1,0},{2,3},{3,2},{4,5},{5,4},{6,7},{7,6},{8,9},{9,8},{10,11... | collective-permute-start | bytes 786440 | tf_op jit(solution)/shard_map/ppermute | solution.py:101
  17.0 0.0 collective-permute-done.13.refs_16_
  17.0 0.1 collective-permute-start.3
  17.0 4.8 %collective-permute-done.6.refs_7_ = bf16[128,1024]{1,0:T(8,128)(2,1)S(1)} collective-permute-done((bf16[128,1024]{1,0:T(8,128)(2,1)S(1)}, bf16[128,1024]{1,0:T(8,128)(2,1)S(1)}, u32[]{:S(2)}, u32[]{:S(2)}) %collective-permute-start.6) | collective-permute-done | bytes 262176 | tf_op jit(solution)/shard_map/ppermute | solution.py:101
  21.8 0.0 collective-permute-start.7
  21.8 1.2 %collective-permute-done.4.refs_5_ = bf16[128,1024]{1,0:T(8,128)(2,1)S(1)} collective-permute-done((bf16[128,1024]{1,0:T(8,128)(2,1)S(1)}, bf16[128,1024]{1,0:T(8,128)(2,1)S(1)}, u32[]{:S(2)}, u32[]{:S(2)}) %collective-permute-start.4) | collective-permute-done | bytes 262176 | tf_op jit(solution)/shard_map/ppermute | solution.py:101
  23.0 0.2 collective-permute-start.5
  23.2 0.0 collective-permute-done.10.refs_12_
  23.2 0.0 collective-permute-done.1.refs_2_
  23.2 0.0 collective-permute-done.3.refs_4_
  23.2 0.1 collective-permute-done.7.refs_8_
  23.4 1.2 %collective-permute-done.5.refs_6_ = bf16[128,1024]{1,0:T(8,128)(2,1)S(1)} collective-permute-done((bf16[128,1024]{1,0:T(8,128)(2,1)S(1)}, bf16[128,1024]{1,0:T(8,128)(2,1)S(1)}, u32[]{:S(2)}, u32[]{:S(2)}) %collective-permute-start.5) | collective-permute-done | bytes 262176 | tf_op jit(solution)/shard_map/ppermute | solution.py:101
  24.6 4.7 %group_softmax.1 = (f32[128]{0:T(128)}, bf16[128,1024]{1,0:T(8,128)(2,1)}, bf16[128,1024]{1,0:T(8,128)(2,1)}) custom-call(bf16[128,1024]{1,0:T(8,128)(2,1)} %refs_0_.1, bf16[128,1024]{1,0:T(8,128)(2,1)S(1)} %collective-permute-done.refs_1_, bf16[128,1024]{1,0:T(8,128)(2,1)S(1)} %collective-permute-done.1.refs_2_, ...), custom_call_target="tpu_custom_call" | custom-call | tf_op jit(solution)/shard_map/group_softmax/pallas_call | solution.py:123
Async XLA Ops:
  0.6 6.2 %collective-permute-start.11 = (bf16[128,1024]{1,0:T(8,128)(2,1)}, bf16[128,1024]{1,0:T(8,128)(2,1)S(1)}, u32[]{:S(2)}, u32[]{:S(2)}) collective-permute-start(bf16[128,1024]{1,0:T(8,128)(2,1)} %refs_13_.1), channel_id=1, source_target_pairs={{0,1},{1,0},{2,3},{3,2},{4,5},{5,4},{6,7},{7,6},{8,9},{9,8},{10,11... | collective-permute-start | bytes 786440 | tf_op jit(solution)/shard_map/ppermute | solution.py:101
  1.1 9.9 %collective-permute-start.12 = (bf16[128,1024]{1,0:T(8,128)(2,1)}, bf16[128,1024]{1,0:T(8,128)(2,1)S(1)}, u32[]{:S(2)}, u32[]{:S(2)}) collective-permute-start(bf16[128,1024]{1,0:T(8,128)(2,1)} %refs_13_.1), channel_id=1, source_target_pairs={{0,2},{1,3},{2,0},{3,1},{4,6},{5,7},{6,4},{7,5},{8,10},{9,11},{10,... | collective-permute-start | bytes 786440 | tf_op jit(solution)/shard_map/ppermute | solution.py:101
  3.7 9.4 %collective-permute-start = (bf16[128,1024]{1,0:T(8,128)(2,1)}, bf16[128,1024]{1,0:T(8,128)(2,1)S(1)}, u32[]{:S(2)}, u32[]{:S(2)}) collective-permute-start(bf16[128,1024]{1,0:T(8,128)(2,1)} %refs_0_.1), channel_id=1, source_target_pairs={{0,16},{1,9},{2,18},{3,11},{4,20},{5,13},{6,22},{7,15},{8,24},{9,1... | collective-permute-start | bytes 786440 | tf_op jit(solution)/shard_map/ppermute | solution.py:101
  6.3 8.6 %collective-permute-start.8 = (bf16[128,1024]{1,0:T(8,128)(2,1)}, bf16[128,1024]{1,0:T(8,128)(2,1)S(1)}, u32[]{:S(2)}, u32[]{:S(2)}) collective-permute-start(bf16[128,1024]{1,0:T(8,128)(2,1)} %refs_9_.1), channel_id=1, source_target_pairs={{0,1},{1,0},{2,3},{3,2},{4,5},{5,4},{6,7},{7,6},{8,9},{9,8},{10,11... | collective-permute-start | bytes 786440 | tf_op jit(solution)/shard_map/ppermute | solution.py:101
  6.3 10.1 %collective-permute-start.9 = (bf16[128,1024]{1,0:T(8,128)(2,1)}, bf16[128,1024]{1,0:T(8,128)(2,1)S(1)}, u32[]{:S(2)}, u32[]{:S(2)}) collective-permute-start(bf16[128,1024]{1,0:T(8,128)(2,1)} %refs_9_.1), channel_id=1, source_target_pairs={{0,2},{1,3},{2,0},{3,1},{4,6},{5,7},{6,4},{7,5},{8,10},{9,11},{10,... | collective-permute-start | bytes 786440 | tf_op jit(solution)/shard_map/ppermute | solution.py:101
  6.8 9.6 %collective-permute-start.2 = (bf16[128,1024]{1,0:T(8,128)(2,1)}, bf16[128,1024]{1,0:T(8,128)(2,1)S(1)}, u32[]{:S(2)}, u32[]{:S(2)}) collective-permute-start(bf16[128,1024]{1,0:T(8,128)(2,1)} %refs_0_.1), channel_id=1, source_target_pairs={{0,0},{1,5},{2,2},{3,7},{4,4},{5,1},{6,6},{7,3},{8,8},{9,13},{10,1... | collective-permute-start | bytes 786440 | tf_op jit(solution)/shard_map/ppermute | solution.py:101
  11.1 5.9 %collective-permute-start.13 = (bf16[128,1024]{1,0:T(8,128)(2,1)S(1)}, bf16[128,1024]{1,0:T(8,128)(2,1)S(1)}, u32[]{:S(2)}, u32[]{:S(2)}) collective-permute-start(bf16[128,1024]{1,0:T(8,128)(2,1)S(1)} %collective-permute-done.12.refs_15_), channel_id=1, source_target_pairs={{0,1},{1,0},{2,3},{3,2},{4,5},{5,4},{6,7},{7,6},{8,9},{9,8},{10,11... | collective-permute-start | bytes 786440 | tf_op jit(solution)/shard_map/ppermute | solution.py:101
  13.1 8.7 %collective-permute-start.6 = (bf16[128,1024]{1,0:T(8,128)(2,1)S(1)}, bf16[128,1024]{1,0:T(8,128)(2,1)S(1)}, u32[]{:S(2)}, u32[]{:S(2)}) collective-permute-start(bf16[128,1024]{1,0:T(8,128)(2,1)S(1)} %collective-permute-done.refs_1_), channel_id=1, source_target_pairs={{0,8},{1,5},{2,10},{3,7},{4,12},{5,1},{6,14},{7,3},{8,0},{9,13},{1... | collective-permute-start | bytes 786440 | tf_op jit(solution)/shard_map/ppermute | solution.py:101
  14.9 8.2 %collective-permute-start.4 = (bf16[128,1024]{1,0:T(8,128)(2,1)S(1)}, bf16[128,1024]{1,0:T(8,128)(2,1)S(1)}, u32[]{:S(2)}, u32[]{:S(2)}) collective-permute-start(bf16[128,1024]{1,0:T(8,128)(2,1)S(1)} %collective-permute-done.refs_1_), channel_id=1, source_target_pairs={{0,4},{1,21},{2,6},{3,23},{4,0},{5,17},{6,2},{7,19},{8,12},{9,29},... | collective-permute-start | bytes 786440 | tf_op jit(solution)/shard_map/ppermute | solution.py:101
  16.4 6.8 %collective-permute-start.1 = (bf16[128,1024]{1,0:T(8,128)(2,1)S(1)}, bf16[128,1024]{1,0:T(8,128)(2,1)S(1)}, u32[]{:S(2)}, u32[]{:S(2)}) collective-permute-start(bf16[128,1024]{1,0:T(8,128)(2,1)S(1)} %collective-permute-done.refs_1_), channel_id=1, source_target_pairs={{0,1},{1,0},{2,3},{3,2},{4,5},{5,4},{6,7},{7,6},{8,9},{9,8},{10,11... | collective-permute-start | bytes 786440 | tf_op jit(solution)/shard_map/ppermute | solution.py:101
  16.4 6.8 %collective-permute-start.10 = (bf16[128,1024]{1,0:T(8,128)(2,1)S(1)}, bf16[128,1024]{1,0:T(8,128)(2,1)S(1)}, u32[]{:S(2)}, u32[]{:S(2)}) collective-permute-start(bf16[128,1024]{1,0:T(8,128)(2,1)S(1)} %collective-permute-done.9.refs_11_), channel_id=1, source_target_pairs={{0,1},{1,0},{2,3},{3,2},{4,5},{5,4},{6,7},{7,6},{8,9},{9,8},{10,11... | collective-permute-start | bytes 786440 | tf_op jit(solution)/shard_map/ppermute | solution.py:101
  17.0 6.3 %collective-permute-start.3 = (bf16[128,1024]{1,0:T(8,128)(2,1)S(1)}, bf16[128,1024]{1,0:T(8,128)(2,1)S(1)}, u32[]{:S(2)}, u32[]{:S(2)}) collective-permute-start(bf16[128,1024]{1,0:T(8,128)(2,1)S(1)} %collective-permute-done.2.refs_3_), channel_id=1, source_target_pairs={{0,1},{1,0},{2,3},{3,2},{4,5},{5,4},{6,7},{7,6},{8,9},{9,8},{10,11... | collective-permute-start | bytes 786440 | tf_op jit(solution)/shard_map/ppermute | solution.py:101
  21.8 1.5 %collective-permute-start.7 = (bf16[128,1024]{1,0:T(8,128)(2,1)S(1)}, bf16[128,1024]{1,0:T(8,128)(2,1)S(1)}, u32[]{:S(2)}, u32[]{:S(2)}) collective-permute-start(bf16[128,1024]{1,0:T(8,128)(2,1)S(1)} %collective-permute-done.6.refs_7_), channel_id=1, source_target_pairs={{0,1},{1,0},{2,3},{3,2},{4,5},{5,4},{6,7},{7,6},{8,9},{9,8},{10,11... | collective-permute-start | bytes 786440 | tf_op jit(solution)/shard_map/ppermute | solution.py:101
  23.0 1.5 %collective-permute-start.5 = (bf16[128,1024]{1,0:T(8,128)(2,1)S(1)}, bf16[128,1024]{1,0:T(8,128)(2,1)S(1)}, u32[]{:S(2)}, u32[]{:S(2)}) collective-permute-start(bf16[128,1024]{1,0:T(8,128)(2,1)S(1)} %collective-permute-done.4.refs_5_), channel_id=1, source_target_pairs={{0,1},{1,0},{2,3},{3,2},{4,5},{5,4},{6,7},{7,6},{8,9},{9,8},{10,11... | collective-permute-start | bytes 786440 | tf_op jit(solution)/shard_map/ppermute | solution.py:101
